TPU v7x, 128 devices: a whole 4x4x4 slice. The times are simulated.
128 devices in a mesh: lat: 8 (over x, z_hi), lon: 16 (over y, z_lo, core).
Axes of the slice: x: 4, y: 4, z: 4 (z_hi: 2, z_lo: 2; z = z_hi * 2 + z_lo), core: 2. Of those that a mesh axis runs over, the one named last changes fastest.
Arguments:
- ocean_state: bfloat16 [256, 4096, 128], P('lat', 'lon'), may hold values from -6 to 6
- sea_mask: int32 [256, 4096], P('lat', 'lon'), may hold values from 0 to 1, as said below
- depth_kernel: bfloat16 [7, 7, 128], replicated, may hold values from -0.875 to 0.875
- conv_bias: float32 [128], replicated, may hold values from -3 to 3
- norm_gain: float32 [128], replicated, may hold values from 0.5 to 1.5
- w_in: bfloat16 [128, 512], replicated, may hold values from -0.5 to 0.5
- w_out: bfloat16 [512, 128], replicated, may hold values from -0.25 to 0.25
- cotangent: bfloat16 [256, 4096, 128], P('lat', 'lon'), may hold values from -6 to 6
Outputs:
- updated: bfloat16 [256, 4096, 128], P('lat', 'lon')
- grad_state: bfloat16 [256, 4096, 128], P('lat', 'lon')
- grad_kernel: float32 [7, 7, 128], replicated
- grad_bias: float32 [128], replicated
- grad_gain: float32 [128], replicated
- grad_w_in: float32 [128, 512], replicated
- grad_w_out: float32 [512, 128], replicated
Inputs may be any that keep to these rules, and one draw needn't show every extreme that they name: `sea_mask`: 1 marks an ocean cell. The tile of one device (32 x 256 cells) holds 6144, 3072 or 768 ocean cells; at each index of lat a quarter of the lon indices have tiles with 6144, a quarter with 3072 and the rest with 768, so each row of tiles holds 43008 ocean cells.
All inputs are finite; a program needn't handle non-finite values.
Results may differ from a plain program's by a relative error of at most 0.014.
Values may be sent and summed in bfloat16 or wider, within the bound.
A program may use at most 128 MiB of HBM per device.

v0:
```python
import jax
import jax.numpy as jnp
from jax import lax
from jax.sharding import PartitionSpec as P

epsilon = 1e-06
root_half = 0.7978845608028654
cubic_coef = 0.044715


def partner(value, axis, apart):
    mask = 2**apart
    pairs = [(source, source ^ mask) for source in range(lax.axis_size(axis))]
    return lax.ppermute(value, axis, pairs)


def with_halo(block, sides, width, periodic):
    for axis, dim in sides:
        count = lax.axis_size(axis)
        forward = [(i, i + 1) for i in range(count - 1)]
        if periodic:
            forward.append((count - 1, 0))
        backward = [(target, source) for source, target in forward]
        low = lax.ppermute(
            lax.slice_in_dim(block, block.shape[dim] - width, None, axis=dim), axis, forward
        )
        high = lax.ppermute(lax.slice_in_dim(block, 0, width, axis=dim), axis, backward)
        block = jnp.concatenate([low, block, high], axis=dim)
    return block


def gelu_pair(preact):
    inner_arg = root_half * (preact + cubic_coef * preact * preact * preact)
    tanh_val = jnp.tanh(inner_arg)
    active = 0.5 * preact * (1.0 + tanh_val)
    derivative = 0.5 * (1.0 + tanh_val) + 0.5 * preact * (1.0 - tanh_val * tanh_val) * root_half * (
        1.0 + 3.0 * cubic_coef * preact * preact
    )
    return (active, derivative)


def normalize(conv_rows, norm_gain):
    centre = jnp.mean(conv_rows, axis=-1, keepdims=True)
    shifted = conv_rows - centre
    variance = jnp.mean(shifted * shifted, axis=-1, keepdims=True)
    inv_std = 1.0 / jnp.sqrt(variance + epsilon)
    unit_norm = shifted * inv_std
    return (unit_norm, inv_std, (unit_norm * norm_gain).astype(jnp.bfloat16))


def column_mlp(normed, upstream, w_in, w_out):
    preact = jnp.dot(normed, w_in, preferred_element_type=jnp.float32)
    active, derivative = gelu_pair(preact)
    hidden = active.astype(jnp.bfloat16)
    mixed_out = jnp.dot(hidden, w_out, preferred_element_type=jnp.float32).astype(jnp.bfloat16)
    back_hidden = lax.dot_general(
        upstream, w_out, (((1,), (1,)), ((), ())), preferred_element_type=jnp.float32
    )
    back_pre = (back_hidden * derivative).astype(jnp.bfloat16)
    back_normed = lax.dot_general(
        back_pre, w_in, (((1,), (1,)), ((), ())), preferred_element_type=jnp.float32
    ).astype(jnp.bfloat16)
    in_part = lax.dot_general(
        normed, back_pre, (((0,), (0,)), ((), ())), preferred_element_type=jnp.float32
    )
    out_part = lax.dot_general(
        hidden, upstream, (((0,), (0,)), ((), ())), preferred_element_type=jnp.float32
    )
    return (mixed_out, back_normed, in_part, out_part)


def norm_back(back_normed, unit_norm, inv_std, norm_gain):
    back_float = back_normed.astype(jnp.float32)
    scaled = back_float * norm_gain
    mean_one = jnp.mean(scaled, axis=-1, keepdims=True)
    mean_two = jnp.mean(scaled * unit_norm, axis=-1, keepdims=True)
    back_conv = ((scaled - mean_one - unit_norm * mean_two) * inv_std).astype(jnp.bfloat16)
    gain_part = jnp.sum(back_float * unit_norm, axis=0)
    return (back_conv, gain_part)


def depthwise(extended, tap_block, out_rows, out_cols):
    running = jnp.zeros((out_rows, out_cols, extended.shape[2]), jnp.float32)
    for row_tap in range(7):
        for col_tap in range(7):
            window = extended[row_tap : row_tap + out_rows, col_tap : col_tap + out_cols].astype(
                jnp.float32
            )
            running = running + window * tap_block[row_tap, col_tap].astype(jnp.float32)
    return running


def mirror(edge_rows):
    for bit_index in range(lax.axis_size("lon").bit_length() - 1):
        edge_rows = partner(edge_rows.astype(jnp.bfloat16), "lon", bit_index).astype(
            edge_rows.dtype
        )
    return edge_rows


def add_rims(tile, upper_fill, is_top):
    tile_rows = tile.shape[0]
    stacked = with_halo(tile, (("lat", 0),), 3, False)
    upper_rows = jnp.where(is_top, upper_fill, stacked[tile_rows + 3 :])
    stacked = jnp.concatenate([stacked[: tile_rows + 3], upper_rows], axis=0)
    return with_halo(stacked, (("lon", 1),), 3, True)


def body(ocean_state, sea_mask, depth_kernel, conv_bias, norm_gain, w_in, w_out, cotangent):
    tile_rows, tile_cols, channels = ocean_state.shape
    tile_cells = tile_rows * tile_cols
    is_top = lax.axis_index("lat") == lax.axis_size("lat") - 1
    top_rows = ocean_state[tile_rows - 3 :][::-1, ::-1].astype(jnp.float32)
    extended = add_rims(ocean_state, mirror(top_rows).astype(jnp.bfloat16), is_top)
    conv_out = depthwise(extended, depth_kernel, tile_rows, tile_cols) + conv_bias
    unit_norm, inv_std, normed = normalize(conv_out.reshape(tile_cells, channels), norm_gain)
    sea_flat = sea_mask.reshape(tile_cells)
    sea_column = (sea_flat == 1)[:, None]
    cot_flat = cotangent.reshape(tile_cells, channels)
    upstream = jnp.where(sea_column, cot_flat, jnp.zeros_like(cot_flat))
    mixed_out, back_normed, in_part, out_part = column_mlp(normed, upstream, w_in, w_out)
    mixed_float = jnp.where(sea_column, mixed_out.astype(jnp.float32), 0.0).reshape(
        tile_rows, tile_cols, channels
    )
    updated = (ocean_state.astype(jnp.float32) + mixed_float).astype(jnp.bfloat16)
    back_conv, gain_part = norm_back(back_normed, unit_norm, inv_std, norm_gain)
    back_tile = back_conv.reshape(tile_rows, tile_cols, channels)
    back_ext = add_rims(back_tile, jnp.zeros((3, tile_cols, channels), jnp.bfloat16), is_top)
    top_slab = jnp.concatenate(
        [back_ext[tile_rows:], jnp.zeros((3, tile_cols + 6, channels), jnp.bfloat16)], axis=0
    )
    back_float = back_tile.astype(jnp.float32)
    inner_grad = jnp.zeros((tile_rows, tile_cols, channels), jnp.float32)
    fold_val = jnp.zeros((3, tile_cols, channels), jnp.float32)
    kernel_rows = []
    for row_tap in range(7):
        kernel_cols = []
        for col_tap in range(7):
            weight_tap = depth_kernel[row_tap, col_tap].astype(jnp.float32)
            inner_grad = (
                inner_grad
                + back_ext[
                    6 - row_tap : 6 - row_tap + tile_rows, 6 - col_tap : 6 - col_tap + tile_cols
                ].astype(jnp.float32)
                * weight_tap
            )
            fold_val = (
                fold_val
                + top_slab[6 - row_tap : 9 - row_tap, 6 - col_tap : 6 - col_tap + tile_cols].astype(
                    jnp.float32
                )
                * weight_tap
            )
            window = extended[row_tap : row_tap + tile_rows, col_tap : col_tap + tile_cols].astype(
                jnp.float32
            )
            kernel_cols.append(jnp.sum(window * back_float, axis=(0, 1)))
        kernel_rows.append(jnp.stack(kernel_cols))
    kernel_grad = jnp.stack(kernel_rows)
    returned = jnp.where(is_top, mirror(fold_val[::-1, ::-1]), 0.0)
    state_grad = cotangent.astype(jnp.float32) + inner_grad
    state_grad = jnp.concatenate(
        [state_grad[: tile_rows - 3], state_grad[tile_rows - 3 :] + returned], axis=0
    ).astype(jnp.bfloat16)
    bias_grad = jnp.sum(back_conv.astype(jnp.float32), axis=0)
    grid_cells = tile_cells * lax.axis_size("lat") * lax.axis_size("lon")
    grad_scale = 1.0 / jnp.sqrt(jnp.float32(grid_cells))
    grad_totals = lax.psum((kernel_grad, bias_grad, gain_part, in_part, out_part), ("lat", "lon"))
    return (
        updated,
        state_grad,
        grad_totals[0] * grad_scale,
        grad_totals[1] * grad_scale,
        grad_totals[2] * grad_scale,
        grad_totals[3] * grad_scale,
        grad_totals[4] * grad_scale,
    )


def solution(mesh):
    return jax.shard_map(
        body,
        mesh=mesh,
        in_specs=(
            P("lat", "lon", None),
            P("lat", "lon"),
            P(),
            P(),
            P(),
            P(),
            P(),
            P("lat", "lon", None),
        ),
        out_specs=(P("lat", "lon", None), P("lat", "lon", None), P(), P(), P(), P(), P()),
        check_vma=False,
    )
```

profile of v0, /device:TPU:1, one launch (start us, length us, event | category | flops | bytes accessed | tf_op | source)
XLA Modules:
  0.0 430.7 jit_solution(3156066651984733778)
XLA Ops:
  8.4 6.3 %collective-permute-start = (bf16[3,256,128]{2,1,0:T(8,128)(2,1)S(1)}, bf16[3,256,128]{2,1,0:T(8,128)(2,1)S(1)}, u32[]{:S(2)}, u32[]{:S(2)}) collective-permute-start(bf16[3,256,128]{2,1,0:T(8,128)(2,1)S(1)} %get-tuple-element.89), channel_id=1, source_target_pairs={{0,16},{16,32},{32,48},{48,64},{64,80},{80,96},{96,112},{1,17},{17... | collective-permute-start | bytes 589832 | tf_op jit(solution)/shard_map/ppermute | solution.py:24
  18.1 6.6 %bitcast_select_fusion = bf16[8192,128]{1,0:T(8,128)(2,1)} fusion(bf16[32,256,128]{2,1,0:T(8,128)(2,1)} %param.15, pred[8192]{0:T(1024)(128)(4,1)S(1)} %eq.18), kind=kLoop, calls=%fused_computation.278 | loop fusion | flops 1048576 | bytes 4202496 | tf_op jit(solution)/shard_map/jit(_where)/select_n | solution.py:120
  25.8 5.8 %collective-permute-done.2 = bf16[3,256,128]{2,1,0:T(8,128)(2,1)S(1)} collective-permute-done((bf16[3,256,128]{2,1,0:T(8,128)(2,1)}, bf16[3,256,128]{2,1,0:T(8,128)(2,1)S(1)}, u32[]{:S(2)}, u32[]{:S(2)}) %collective-permute-start.2) | collective-permute-done | bytes 196640 | tf_op jit(solution)/shard_map/ppermute | solution.py:14
  33.0 4.3 %collective-permute-done.3 = bf16[3,256,128]{2,1,0:T(8,128)(2,1)} collective-permute-done((bf16[3,256,128]{2,1,0:T(8,128)(2,1)S(1)}, bf16[3,256,128]{2,1,0:T(8,128)(2,1)}, u32[]{:S(2)}, u32[]{:S(2)}) %collective-permute-start.3) | collective-permute-done | bytes 196640 | tf_op jit(solution)/shard_map/ppermute | solution.py:14
  37.3 2.9 collective-permute-start.4
  40.8 2.7 collective-permute-done.4
  43.6 3.5 collective-permute-start.6
  48.2 3.1 collective-permute-done.7
  51.3 3.3 maximum_maximum_fusion
  54.9 37.1 %fusion.154 = (f32[32,256]{1,0:T(8,128)S(1)}, f32[32,256,128]{2,1,0:T(8,128)S(1)}) fusion(f32[128]{0:T(128)S(1)} %copy-done.72, f32[128]{0:T(128)S(1)} %get-tuple-element.139, bf16[38,259,128]{2,1,0:T(8,128)(2,1)S(1)} %get-tuple-element.82, f32[128]{0:T(128)S(1)} %get-tuple-element.140, f32[128]{0:T(128)S(1)} %get-tuple-element.93, ...), kind=kLoop, calls=%fused_computation.372 | loop fusion | flops 158326784 | bytes 100918272 | tf_op jit(solution)/shard_map/reduce_sum | solution.py:43
  92.0 2.6 multiply_reduce_fusion.2
  94.7 4.6 %multiply_convert_fusion.2 = bf16[8192,128]{1,0:T(8,128)(2,1)S(1)} fusion(f32[32,256,128]{2,1,0:T(8,128)S(1)} %get-tuple-element.76, f32[128]{0:T(128)S(1)} %copy-done.70, f32[8192]{0:T(1024)S(1)} %bitcast.322, f32[8192]{0:T(1024)S(1)} %bitcast.325), kind=kLoop, calls=%fused_computation.249 | loop fusion | flops 4194304 | bytes 6357504 | tf_op jit(solution)/shard_map/convert_element_type | solution.py:48
  99.3 11.1 %multiply_convert_fusion = (bf16[8192,512]{1,0:T(8,128)(2,1)}, f32[8192,512]{1,0:T(8,128)}) fusion(bf16[8192,128]{1,0:T(8,128)(2,1)S(1)} %multiply_convert_fusion.2, bf16[128,512]{1,0:T(8,128)(2,1)S(1)} %copy-done), kind=kOutput, calls=%fused_computation.59 | convolution fusion | flops 1111490560 | bytes 27394048 | tf_op jit(solution)/shard_map/dot_general | solution.py:52
  110.4 13.5 %fusion.6 = bf16[8192,512]{1,0:T(8,128)(2,1)S(1)} fusion(f32[8192,512]{1,0:T(8,128)} %get-tuple-element.143, bf16[8192,128]{1,0:T(8,128)(2,1)S(1)} %copy-done.11, bf16[512,128]{1,0:T(8,128)(2,1)S(1)} %copy-done.73), kind=kOutput, calls=%fused_computation.58 | convolution fusion | flops 1153433600 | bytes 27394048 | tf_op jit(solution)/shard_map/dot_general | solution.py:56
  124.0 2.0 fusion.158
  126.0 5.3 %multiply_reduce_fusion = (f32[128]{0:T(128)}, f32[8192]{0:T(1024)S(1)}, f32[8192]{0:T(1024)S(1)}, f32[8192,128]{1,0:T(8,128)S(1)}) fusion(f32[32,256,128]{2,1,0:T(8,128)S(1)} %get-tuple-element.76, f32[8192]{0:T(1024)S(1)} %bitcast.323, f32[8192]{0:T(1024)S(1)} %bitcast.326, f32[128]{0:T(128)S(1)} %copy-done.70, bf16[8192,512]{1,0:T(8,128)(2,1)S(1)} %fusion.6, ...), kind=kOutput, calls=%fused_computation.244 | convolution fusion | flops 1084211072 | bytes 17040384 | tf_op jit(solution)/shard_map/dot_general | solution.py:60
  131.2 6.7 %convert_reduce_fusion = (f32[128]{0:T(128)}, bf16[8192,128]{1,0:T(8,128)(2,1)S(1)}) fusion(f32[8192]{0:T(1024)S(1)} %get-tuple-element.144, f32[8192]{0:T(1024)S(1)} %bitcast.324, f32[8192]{0:T(1024)S(1)} %bitcast.327, f32[32,256,128]{2,1,0:T(8,128)S(1)} %get-tuple-element.76, f32[8192]{0:T(1024)S(1)} %get-tuple-element.145, ...), kind=kLoop, calls=%fused_computation.245 | loop fusion | flops 10485632 | bytes 10617856 | tf_op jit(solution)/shard_map/reduce_sum | solution.py:165
  137.9 9.9 %fusion.128 = (f32[128]{0:T(128)S(1)}, f32[128]{0:T(128)S(1)}, f32[128]{0:T(128)S(1)}, f32[128]{0:T(128)S(1)}, f32[128]{0:T(128)S(1)}, /*index=5*/f32[128]{0:T(1...) fusion(bf16[38,259,128]{2,1,0:T(8,128)(2,1)S(1)} %get-tuple-ele, ...), kind=kLoop, calls=%fused_computation.237 | loop fusion | flops 57669376 | bytes 39855104 | tf_op jit(solution)/shard_map/reduce_sum | solution.py:157
  147.9 11.6 %fusion.132 = (f32[128]{0:T(128)S(1)}, f32[128]{0:T(128)S(1)}, f32[128]{0:T(128)S(1)}, f32[128]{0:T(128)S(1)}, f32[128]{0:T(128)S(1)}, /*index=5*/f32[128]{0:T(1...) fusion(bf16[38,259,128]{2,1,0:T(8,128)(2,1)S(1)} %get-tuple-ele, ...), kind=kLoop, calls=%fused_computation.241 | loop fusion | flops 57669376 | bytes 39855104 | tf_op jit(solution)/shard_map/reduce_sum | solution.py:157
  159.5 3.1 fusion.159
  162.5 19.4 %fusion.129 = (f32[128]{0:T(128)}, f32[128]{0:T(128)}, f32[128]{0:T(128)}, f32[128]{0:T(128)}, f32[128]{0:T(128)S(1)}, /*index=5*/f32[128]{0:T(128)S(1)}, f32[12...) fusion(bf16[3,256,128]{2,1,0:T(8,128)(2,1)S(1)} %broadcast_sele, ...), kind=kOutput, calls=%fused_computation.238 | convolution fusion | flops 1124071808 | bytes 33896960 | tf_op jit(solution)/shard_map/dot_general | solution.py:55
  184.5 6.3 %collective-permute-start.8 = (bf16[3,256,128]{2,1,0:T(8,128)(2,1)S(1)}, bf16[3,256,128]{2,1,0:T(8,128)(2,1)S(1)}, u32[]{:S(2)}, u32[]{:S(2)}) collective-permute-start(bf16[3,256,128]{2,1,0:T(8,128)(2,1)S(1)} %bitcast.320), channel_id=1, source_target_pairs={{0,16},{16,32},{32,48},{48,64},{64,80},{80,96},{96,112},{1,17},{17... | collective-permute-start | bytes 589832 | tf_op jit(solution)/shard_map/ppermute | solution.py:24
  194.9 67.8 %all-reduce.1 = (f32[7,7,128]{2,1,0:T(8,128)S(1)}, f32[128]{0:T(128)}, f32[128]{0:T(128)S(1)}) all-reduce(f32[7,7,128]{2,1,0:T(8,128)S(1)} %constant_dynamic-update-slice_fusion.2, f32[128]{0:T(128)} %get-tuple-element.73, f32[128]{0:T(128)} %get-tuple-element.7), channel_id=1, replica_groups=mesh['lat'=8,'lon'=16] {'lat','lon'}, use_global_device_ids=true, to_apply=%region_53.54 | all-reduce | flops 6528 | bytes 52224 | tf_op jit(solution)/shard_map/psum | solution.py:168
  268.5 3.1 pad_maximum_fusion.1
  273.3 2.6 multiply_add_fusion.1
  276.2 3.8 collective-permute-start.12
  281.1 48.6 %convert_add_fusion.1 = f32[32,256,128]{2,1,0:T(8,128)S(1)} fusion(bf16[32,256,128]{2,1,0:T(8,128)(2,1)} %param.15, bf16[32,256,128]{2,1,0:T(8,128)(2,1)} %bitcast.316, bf16[3,256,128]{2,1,0:T(8,128)(2,1)S(1)} %collective-permute-done.8, bf16[3,256,128]{2,1,0:T(8,128)(2,1)S(1)} %broadcast_select_fusion, bf16[38,259,128]{2,1,0:T(8,128)(2,1)} %copy-done.3, ...), kind=kLoop, calls=%fused_computation.248 | loop fusion | flops 161480704 | bytes 96887296 | tf_op jit(solution)/shard_map/add | solution.py:161
  329.6 1.9 copy-done.10
  332.0 79.3 %all-reduce.5.cloned.1.call-done = (f32[128,512]{1,0:T(8,128)}, f32[512,128]{1,0:T(8,128)}) async-done(((f32[128,512]{1,0:T(8,128)}, f32[512,128]{1,0:T(8,128)}), (f32[128,512]{1,0:T(8,128)}, f32[512,128]{1,0:T(8,128)})) %all-reduce.5.cloned.1.call-update) | async-done | bytes 524304 | tf_op jit(solution)/shard_map/psum | solution.py:168
  413.0 2.1 collective-permute-start.15
  415.0 1.7 broadcast_multiply_fusion.1
  416.7 4.3 %collective-permute-done.15 = bf16[3,256,128]{2,1,0:T(8,128)(2,1)S(1)} collective-permute-done((bf16[3,256,128]{2,1,0:T(8,128)(2,1)S(1)}, bf16[3,256,128]{2,1,0:T(8,128)(2,1)S(1)}, u32[]{:S(2)}, u32[]{:S(2)}) %collective-permute-start.15) | collective-permute-done | bytes 196640 | tf_op jit(solution)/shard_map/ppermute | solution.py:14
  (220 shorter events, 28.3 us)
Async XLA Ops:
  7.2 92.1 %copy-start = (bf16[128,512]{1,0:T(8,128)(2,1)S(1)}, bf16[128,512]{1,0:T(8,128)(2,1)}, u32[]{:S(2)}) copy-start(bf16[128,512]{1,0:T(8,128)(2,1)} %param.13) | copy-start | bytes 393220
  7.2 36.4 %copy-start.7 = (bf16[32,256,128]{2,1,0:T(8,128)(2,1)S(1)}, bf16[32,256,128]{2,1,0:T(8,128)(2,1)}, u32[]{:S(2)}) copy-start(bf16[32,256,128]{2,1,0:T(8,128)(2,1)} %param.8) | copy-start | bytes 6291460
  7.2 404.1 %all-reduce.5.cloned.1.call-start = ((), (), s32[]{:S(2)}) async-start(), calls=%async_computation | async-start | bytes 1048576 | tf_op jit(solution)/shard_map/psum | solution.py:168
  8.4 32.3 %collective-permute-start = (bf16[3,256,128]{2,1,0:T(8,128)(2,1)S(1)}, bf16[3,256,128]{2,1,0:T(8,128)(2,1)S(1)}, u32[]{:S(2)}, u32[]{:S(2)}) collective-permute-start(bf16[3,256,128]{2,1,0:T(8,128)(2,1)S(1)} %get-tuple-element.89), channel_id=1, source_target_pairs={{0,16},{16,32},{32,48},{48,64},{64,80},{80,96},{96,112},{1,17},{17... | collective-permute-start | bytes 589832 | tf_op jit(solution)/shard_map/ppermute | solution.py:24
  15.0 9.7 %collective-permute-start.1 = (bf16[3,256,128]{2,1,0:T(8,128)(2,1)S(1)}, bf16[3,256,128]{2,1,0:T(8,128)(2,1)}, u32[]{:S(2)}, u32[]{:S(2)}) collective-permute-start(bf16[3,256,128]{2,1,0:T(8,128)(2,1)S(1)} %rev.6), channel_id=1, source_target_pairs={{0,1},{1,0},{2,3},{3,2},{4,5},{5,4},{6,7},{7,6},{8,9},{9,8},{10,11... | collective-permute-start | bytes 589832 | tf_op jit(solution)/shard_map/ppermute | solution.py:14
  16.1 24.7 %collective-permute-start.5 = (bf16[3,256,128]{2,1,0:T(8,128)(2,1)S(1)}, bf16[3,256,128]{2,1,0:T(8,128)(2,1)S(1)}, u32[]{:S(2)}, u32[]{:S(2)}) collective-permute-start(bf16[3,256,128]{2,1,0:T(8,128)(2,1)S(1)} %get-tuple-element.88), channel_id=1, source_target_pairs={{16,0},{32,16},{48,32},{64,48},{80,64},{96,80},{112,96},{17,1},{33... | collective-permute-start | bytes 589832 | tf_op jit(solution)/shard_map/ppermute | solution.py:27
  24.7 29.8 %copy-start.13 = (f32[128]{0:T(128)}, f32[128]{0:T(128)S(1)}, u32[]{:S(2)}) copy-start(f32[128]{0:T(128)S(1)} %get-tuple-element.110) | copy-start | bytes 1540
  24.7 29.8 %copy-start.63 = (f32[128]{0:T(128)}, f32[128]{0:T(128)S(1)}, u32[]{:S(2)}) copy-start(f32[128]{0:T(128)S(1)} %get-tuple-element.92) | copy-start | bytes 1540
  24.8 6.8 %collective-permute-start.2 = (bf16[3,256,128]{2,1,0:T(8,128)(2,1)}, bf16[3,256,128]{2,1,0:T(8,128)(2,1)S(1)}, u32[]{:S(2)}, u32[]{:S(2)}) collective-permute-start(bf16[3,256,128]{2,1,0:T(8,128)(2,1)} %collective-permute-done.1), channel_id=1, source_target_pairs={{0,2},{1,3},{2,0},{3,1},{4,6},{5,7},{6,4},{7,5},{8,10},{9,11},{10,... | collective-permute-start | bytes 589832 | tf_op jit(solution)/shard_map/ppermute | solution.py:14
  25.6 29.0 %copy-start.15 = (f32[128]{0:T(128)}, f32[128]{0:T(128)S(1)}, u32[]{:S(2)}) copy-start(f32[128]{0:T(128)S(1)} %get-tuple-element.112) | copy-start | bytes 1540
  25.6 29.0 %copy-start.17 = (f32[128]{0:T(128)}, f32[128]{0:T(128)S(1)}, u32[]{:S(2)}) copy-start(f32[128]{0:T(128)S(1)} %get-tuple-element.113) | copy-start | bytes 1540
  25.6 29.0 %copy-start.19 = (f32[128]{0:T(128)}, f32[128]{0:T(128)S(1)}, u32[]{:S(2)}) copy-start(f32[128]{0:T(128)S(1)} %get-tuple-element.114) | copy-start | bytes 1540
  25.6 29.0 %copy-start.21 = (f32[128]{0:T(128)}, f32[128]{0:T(128)S(1)}, u32[]{:S(2)}) copy-start(f32[128]{0:T(128)S(1)} %get-tuple-element.115) | copy-start | bytes 1540
  25.6 29.0 %copy-start.23 = (f32[128]{0:T(128)}, f32[128]{0:T(128)S(1)}, u32[]{:S(2)}) copy-start(f32[128]{0:T(128)S(1)} %get-tuple-element.116) | copy-start | bytes 1540
  25.6 29.0 %copy-start.25 = (f32[128]{0:T(128)}, f32[128]{0:T(128)S(1)}, u32[]{:S(2)}) copy-start(f32[128]{0:T(128)S(1)} %get-tuple-element.117) | copy-start | bytes 1540
  25.7 29.0 %copy-start.27 = (f32[128]{0:T(128)}, f32[128]{0:T(128)S(1)}, u32[]{:S(2)}) copy-start(f32[128]{0:T(128)S(1)} %get-tuple-element.118) | copy-start | bytes 1540
  31.6 5.7 %collective-permute-start.3 = (bf16[3,256,128]{2,1,0:T(8,128)(2,1)S(1)}, bf16[3,256,128]{2,1,0:T(8,128)(2,1)}, u32[]{:S(2)}, u32[]{:S(2)}) collective-permute-start(bf16[3,256,128]{2,1,0:T(8,128)(2,1)S(1)} %collective-permute-done.2), channel_id=1, source_target_pairs={{0,4},{1,5},{2,6},{3,7},{4,0},{5,1},{6,2},{7,3},{8,12},{9,13},{10,... | collective-permute-start | bytes 589832 | tf_op jit(solution)/shard_map/ppermute | solution.py:14
  37.3 6.2 %collective-permute-start.4 = (bf16[3,256,128]{2,1,0:T(8,128)(2,1)}, bf16[3,256,128]{2,1,0:T(8,128)(2,1)S(1)}, u32[]{:S(2)}, u32[]{:S(2)}) collective-permute-start(bf16[3,256,128]{2,1,0:T(8,128)(2,1)} %collective-permute-done.3), channel_id=1, source_target_pairs={{0,8},{1,9},{2,10},{3,11},{4,12},{5,13},{6,14},{7,15},{8,0},{9,1},... | collective-permute-start | bytes 589832 | tf_op jit(solution)/shard_map/ppermute | solution.py:14
  43.6 4.6 %collective-permute-start.6 = (bf16[38,3,128]{2,1,0:T(4,128)(2,1)S(1)}, bf16[38,3,128]{2,1,0:T(4,128)(2,1)S(1)}, u32[]{:S(2)}, u32[]{:S(2)}) collective-permute-start(bf16[38,3,128]{2,1,0:T(4,128)(2,1)S(1)} %get-tuple-element.83), channel_id=1, source_target_pairs={{0,1},{1,2},{2,3},{3,4},{4,5},{5,6},{6,7},{7,8},{8,9},{9,10},{10,1... | collective-permute-start | bytes 87560 | tf_op jit(solution)/shard_map/ppermute | solution.py:24
  47.1 4.2 collective-permute-start.7
  47.9 44.1 %copy-start.9 = (bf16[35,256,128]{2,1,0:T(8,128)(2,1)}, bf16[35,256,128]{2,1,0:T(8,128)(2,1)S(1)}, u32[]{:S(2)}) copy-start(bf16[35,256,128]{2,1,0:T(8,128)(2,1)S(1)} %constant_dynamic-update-slice_fusion) | copy-start | bytes 6881284
  54.6 93.3 %copy-start.2 = (bf16[38,259,128]{2,1,0:T(8,128)(2,1)}, bf16[38,259,128]{2,1,0:T(8,128)(2,1)S(1)}, u32[]{:S(2)}) copy-start(bf16[38,259,128]{2,1,0:T(8,128)(2,1)S(1)} %get-tuple-element.82) | copy-start | bytes 7558660
  182.0 85.8 %copy-start.5 = (bf16[8192,128]{1,0:T(8,128)(2,1)S(1)}, bf16[8192,128]{1,0:T(8,128)(2,1)}, u32[]{:S(2)}) copy-start(bf16[8192,128]{1,0:T(8,128)(2,1)} %copy-done.4) | copy-start | bytes 6291460
  183.2 80.2 %collective-permute-start.9 = (bf16[3,256,128]{2,1,0:T(8,128)(2,1)S(1)}, bf16[3,256,128]{2,1,0:T(8,128)(2,1)S(1)}, u32[]{:S(2)}, u32[]{:S(2)}) collective-permute-start(bf16[3,256,128]{2,1,0:T(8,128)(2,1)S(1)} %bitcast.328), channel_id=1, source_target_pairs={{16,0},{32,16},{48,32},{64,48},{80,64},{96,80},{112,96},{17,1},{33... | collective-permute-start | bytes 589832 | tf_op jit(solution)/shard_map/ppermute | solution.py:27
  184.5 78.9 %collective-permute-start.8 = (bf16[3,256,128]{2,1,0:T(8,128)(2,1)S(1)}, bf16[3,256,128]{2,1,0:T(8,128)(2,1)S(1)}, u32[]{:S(2)}, u32[]{:S(2)}) collective-permute-start(bf16[3,256,128]{2,1,0:T(8,128)(2,1)S(1)} %bitcast.320), channel_id=1, source_target_pairs={{0,16},{16,32},{32,48},{48,64},{64,80},{80,96},{96,112},{1,17},{17... | collective-permute-start | bytes 589832 | tf_op jit(solution)/shard_map/ppermute | solution.py:24
  264.3 3.5 collective-permute-start.10
  265.3 2.5 collective-permute-start.11
  276.2 4.9 %collective-permute-start.12 = (bf16[3,256,128]{2,1,0:T(8,128)(2,1)S(1)}, bf16[3,256,128]{2,1,0:T(8,128)(2,1)S(1)}, u32[]{:S(2)}, u32[]{:S(2)}) collective-permute-start(bf16[3,256,128]{2,1,0:T(8,128)(2,1)S(1)} %rev.7), channel_id=1, source_target_pairs={{0,1},{1,0},{2,3},{3,2},{4,5},{5,4},{6,7},{7,6},{8,9},{9,8},{10,11... | collective-permute-start | bytes 589832 | tf_op jit(solution)/shard_map/ppermute | solution.py:14
  281.1 50.8 %collective-permute-start.13 = (bf16[3,256,128]{2,1,0:T(8,128)(2,1)S(1)}, bf16[3,256,128]{2,1,0:T(8,128)(2,1)S(1)}, u32[]{:S(2)}, u32[]{:S(2)}) collective-permute-start(bf16[3,256,128]{2,1,0:T(8,128)(2,1)S(1)} %collective-permute-done.12), channel_id=1, source_target_pairs={{0,2},{1,3},{2,0},{3,1},{4,6},{5,7},{6,4},{7,5},{8,10},{9,11},{10,... | collective-permute-start | bytes 589832 | tf_op jit(solution)/shard_map/ppermute | solution.py:14
  281.1 142.5 %copy-start.1 = (bf16[128,512]{1,0:T(8,128)(2,1)S(1)}, bf16[128,512]{1,0:T(8,128)(2,1)}, u32[]{:S(2)}) copy-start(bf16[128,512]{1,0:T(8,128)(2,1)} %param.13) | copy-start | bytes 393220
  331.9 81.1 %collective-permute-start.14 = (bf16[3,256,128]{2,1,0:T(8,128)(2,1)S(1)}, bf16[3,256,128]{2,1,0:T(8,128)(2,1)S(1)}, u32[]{:S(2)}, u32[]{:S(2)}) collective-permute-start(bf16[3,256,128]{2,1,0:T(8,128)(2,1)S(1)} %collective-permute-done.13), channel_id=1, source_target_pairs={{0,4},{1,5},{2,6},{3,7},{4,0},{5,1},{6,2},{7,3},{8,12},{9,13},{10,... | collective-permute-start | bytes 589832 | tf_op jit(solution)/shard_map/ppermute | solution.py:14
  413.0 8.1 %collective-permute-start.15 = (bf16[3,256,128]{2,1,0:T(8,128)(2,1)S(1)}, bf16[3,256,128]{2,1,0:T(8,128)(2,1)S(1)}, u32[]{:S(2)}, u32[]{:S(2)}) collective-permute-start(bf16[3,256,128]{2,1,0:T(8,128)(2,1)S(1)} %collective-permute-done.14), channel_id=1, source_target_pairs={{0,8},{1,9},{2,10},{3,11},{4,12},{5,13},{6,14},{7,15},{8,0},{9,1},... | collective-permute-start | bytes 589832 | tf_op jit(solution)/shard_map/ppermute | solution.py:14
  (62 other events, 829.2 us)
Sparse Core Ops, SparseCore 0:
  266.8 144.4 all-reduce.4
where the time goes:
time: 434 us; the launch traced here: 431 us
  other arithmetic  147 us (34%)
  waiting for transfers between devices  102 us (24%)
  blocking collectives  67.8 us (16%)
  matrix products  54.4 us (13%)
  starting transfers between devices  33 us (8%)
  between operations  15.6 us (4%)
  local copies, waits for them, and re-layouts  11.7 us (3%)
    psum x1, waiting for transfers between devices, body(): lax.psum((kernel_grad, bias_grad, gain_part, in_part, out_part), ('lat',...  79.3 us
    psum x1, blocking collectives, body(): lax.psum((kernel_grad, bias_grad, gain_part, in_part, out_part), ('lat',...  67.8 us
    add x1, other arithmetic, body(): state_grad = cotangent.astype(jnp.float32) + inner_grad  48.6 us
    reduce_sum x1, other arithmetic, normalize(): centre = jnp.mean(conv_rows, axis=-1, keepdims=True)  37.1 us
    reduce_sum x2, other arithmetic, body(): kernel_cols.append(jnp.sum(window * back_float, axis=(0, 1)))  21.5 us
    dot_general x1, matrix products, column_mlp(): jnp.dot(hidden, w_out, preferred_element_type=jnp.float32)  19.4 us
    ppermute x8, waiting for transfers between devices, partner(): return lax.ppermute(value, axis, pairs)  17.7 us
    ppermute x4, starting transfers between devices, with_halo(): lax.ppermute(lax.slice_in_dim(block, block.shape[dim] - width, None, axis...  17 us
  transfers between devices with their start and end apart: 17, of which 9 were waited for; matrix products, arithmetic and copies ran while one was open for 17% of the time, Pallas kernels for 0%

commit v1 on v0

v1 whole, which is shorter than its diff:
```python
import functools
import jax
import jax.numpy as jnp
from jax import lax
from jax.experimental import pallas as pl
from jax.experimental.pallas import tpu as pltpu
from jax.sharding import PartitionSpec as P

MESH = pl.DeviceIdType.MESH
bf16 = jnp.bfloat16
f32 = jnp.float32
epsilon = 1e-06
root_half = 0.7978845608028654
cubic_coef = 0.044715

C = 128
ROWS = 32
COLS = 256
HID = 512
EXT = 22 * 16
VLIM = 60 * 1024 * 1024


def iota2(shape, dim):
    return lax.broadcasted_iota(jnp.int32, shape, dim)


def one_hot(hit):
    return jnp.where(hit, 1.0, 0.0).astype(bf16)


def place(rows, edges):
    o = iota2((rows, 1), 0)
    if edges:
        o = jnp.where(o >= 48, o + 256, o)
    return (o % 16) * 16 + o // 16 - 3


def swap(o):
    return (o % 16) * 16 + o // 16


def dot(a, b):
    return jnp.dot(a, b, preferred_element_type=f32)


def dot_t(a, b):
    return lax.dot_general(a, b, (((0,), (0,)), ((), ())), preferred_element_type=f32)


def conv_taps(ext, row, taps, k0, nk):
    acc = [None] * nk
    for a in range(7):
        win = [ext[row + a, k0 + kk] for kk in range(nk + 6)]
        w = [taps[a * 7 + b] for b in range(7)]
        for k in range(nk):
            p = win[k] * w[0]
            for b in range(1, 7):
                p = p + win[k + b] * w[b]
            p = p.astype(f32)
            acc[k] = p if acc[k] is None else acc[k] + p
    return acc


def gelu_parts(v):
    u = v * v
    t = jnp.tanh(v * (root_half + (root_half * cubic_coef) * u))
    h = 0.5 * t + 0.5
    act = v * h
    der = h + act * (1.0 - h) * (2.0 * root_half + (6.0 * root_half * cubic_coef) * u)
    return act, der


R = 2
M = R * COLS
NB = ROWS // R


def main_kernel(flags, x, hr, hc, mask, cot, taps1, bias, gain, w_in, w_in_t, w_out, w_out_t,
                upd, back, edge, xp, gin, gout, small,
                ext, taps, perm, norm_s, unit_s, inv_s, up_s, mask_s, xs_s):
    i = pl.program_id(0)

    @pl.when(i == 0)
    def _():
        for t in range(49):
            taps[t] = jnp.broadcast_to(taps1[t:t + 1], (16, C))
        col = iota2((1, COLS), 1)
        amat = one_hot(place(EXT, False) == col)
        h = iota2((1, 32), 1)
        bmat = one_hot(place(96, True) == jnp.where(h < 16, h - 16, 240 + h))
        perm[...] = one_hot(swap(iota2((COLS, 1), 0)) == col)

        def build(am, bm, main, side):
            full = dot(am, main)
            rim = dot(bm, side)
            return jnp.concatenate([full[:48] + rim[:48], full[48:304], full[304:] + rim[48:]], axis=0).astype(bf16)

        def inner(j, _):
            main = jnp.concatenate([x[2 * j], x[2 * j + 1]], axis=-1)
            side = jnp.concatenate([hc[2 * j + 3], hc[2 * j + 4]], axis=-1)
            full = build(amat, bmat, main, side)
            ext[2 * j + 3] = full[:, :C].reshape(22, 16, C)
            ext[2 * j + 4] = full[:, C:].reshape(22, 16, C)
            return 0

        lax.fori_loop(0, ROWS // 2, inner, 0)
        is_bottom = flags[0] == 1
        is_top = flags[1] == 1
        for e in range(3):
            main = jnp.where(is_bottom, jnp.zeros((COLS, C), bf16), hr[e])
            side = jnp.where(is_bottom, jnp.zeros((32, C), bf16), hc[e])
            ext[e] = build(amat, bmat, main, side).reshape(22, 16, C)
        acol = jnp.where(is_top, 255 - col, col)
        amat_t = one_hot(place(EXT, False) == acol)
        hpos = jnp.where(is_top, jnp.where(h < 16, -1 - h, 287 - h), jnp.where(h < 16, h - 16, 240 + h))
        bmat_t = one_hot(place(96, True) == hpos)
        for m in range(3):
            src = jnp.where(is_top, 2 - m, m)
            ext[35 + m] = build(amat_t, bmat_t, hr[3 + src], hc[35 + src]).reshape(22, 16, C)
        norm_s[...] = jnp.zeros_like(norm_s)
        unit_s[...] = jnp.zeros_like(unit_s)
        inv_s[...] = jnp.zeros_like(inv_s)
        up_s[...] = jnp.zeros_like(up_s)
        mask_s[...] = jnp.zeros_like(mask_s)
        xs_s[...] = jnp.zeros_like(xs_s)
        gin[...] = jnp.zeros_like(gin)
        gout[...] = jnp.zeros_like(gout)
        small[...] = jnp.zeros_like(small)

    other = 1 - i % 2
    slot = i % 2
    normed = norm_s[other]
    upstream = up_s[other]
    mixed = None
    bn = None
    for f in range(0, HID, 256):
        pre = dot(normed, w_in[:, f:f + 256])
        bh = dot(upstream, w_out_t[:, f:f + 256])
        act, der = gelu_parts(pre)
        hid = act.astype(bf16)
        bp = (bh * der).astype(bf16)
        mx = dot(hid, w_out[f:f + 256])
        bx = dot(bp, w_in_t[f:f + 256])
        mixed = mx if mixed is None else mixed + mx
        bn = bx if bn is None else bn + bx
        gin[:, f:f + 256] += dot_t(normed, bp)
        gout[:, f:f + 256] += dot_t(upstream, hid)
    mixed = (mixed * mask_s[other]).astype(bf16)
    pm = perm[...]
    unit = unit_s[other]
    bnf = bn.astype(bf16).astype(f32)
    g = bnf * gain[...]
    m1 = jnp.mean(g, axis=-1, keepdims=True)
    m2 = jnp.mean(g * unit, axis=-1, keepdims=True)
    bc = ((g - m1 - unit * m2) * inv_s[other]).astype(bf16)
    small[0:8] += jnp.sum((bnf * unit).reshape(M // 8, 8, C), axis=0)
    small[8:16] += jnp.sum(bc.astype(f32).reshape(M // 8, 8, C), axis=0)
    h32 = iota2((32, 1), 0)
    sel = one_hot(jnp.where(h32 < 16, h32, 224 + h32) == swap(iota2((1, COLS), 1)))
    for r in range(R):
        sl = slice(r * COLS, (r + 1) * COLS)
        nat = dot(pm, mixed[sl])
        upd[r] = (xs_s[other, sl].astype(f32) + nat).astype(bf16)
        back[r] = bc[sl]
        edge[r] = dot(sel, bc[sl]).astype(bf16)

    nb = jnp.minimum(i, NB - 1)
    ones = jnp.ones((COLS, C), bf16)
    for r in range(R):
        row = nb * R + r
        sl = slice(r * COLS, (r + 1) * COLS)
        accs = []
        for k0 in (0, 8):
            accs += conv_taps(ext, row, taps, k0, 8)
        conv = jnp.concatenate([a + bias[...] for a in accs], axis=0)
        centre = jnp.mean(conv, axis=-1, keepdims=True)
        shifted = conv - centre
        var = jnp.mean(shifted * shifted, axis=-1, keepdims=True)
        inv = lax.rsqrt(var + epsilon)
        unit = shifted * inv
        unit_s[slot, sl] = unit
        inv_s[slot, sl] = jnp.broadcast_to(inv, (COLS, C))
        norm_s[slot, sl] = (unit * gain[...]).astype(bf16)
        pmask = pm * mask[pl.ds(row, 1), :].astype(f32).astype(bf16)
        both = dot(pmask, jnp.concatenate([cot[r], ones], axis=-1))
        up_s[slot, sl] = both[:, :C].astype(bf16)
        mask_s[slot, sl] = both[:, C:]
        xs_s[slot, sl] = x[row]
        xp[r] = ext[row + 3, 3:19].reshape(COLS, C)


def main_call(flags, x, hr, hc, mask, cot, depth_kernel, bias, gain, w_in, w_out):
    vm = pl.BlockSpec(memory_space=pltpu.VMEM)
    now = lambda i: (jnp.minimum(i, NB - 1), 0, 0)
    past = lambda i: (jnp.maximum(i - 1, 0), 0, 0)
    whole2 = lambda i: (0, 0)
    tile = jax.ShapeDtypeStruct((ROWS, COLS, C), bf16)
    return pl.pallas_call(
        main_kernel,
        grid=(NB + 1,),
        in_specs=[pl.BlockSpec(memory_space=pltpu.SMEM), vm, vm, vm, vm,
                  pl.BlockSpec((R, COLS, C), now), vm, vm, vm, vm, vm, vm, vm],
        out_specs=[pl.BlockSpec((R, COLS, C), past), pl.BlockSpec((R, COLS, C), past),
                   pl.BlockSpec((R, 32, C), past), pl.BlockSpec((R, COLS, C), now),
                   pl.BlockSpec((C, HID), whole2), pl.BlockSpec((C, HID), whole2), pl.BlockSpec((16, C), whole2)],
        out_shape=[tile, tile, jax.ShapeDtypeStruct((ROWS, 32, C), bf16), tile,
                   jax.ShapeDtypeStruct((C, HID), f32), jax.ShapeDtypeStruct((C, HID), f32),
                   jax.ShapeDtypeStruct((16, C), f32)],
        scratch_shapes=[
            pltpu.VMEM((38, 22, 16, C), bf16), pltpu.VMEM((49, 16, C), bf16), pltpu.VMEM((COLS, COLS), bf16),
            pltpu.VMEM((2, M, C), bf16), pltpu.VMEM((2, M, C), f32), pltpu.VMEM((2, M, C), f32),
            pltpu.VMEM((2, M, C), bf16), pltpu.VMEM((2, M, C), f32), pltpu.VMEM((2, M, C), bf16)],
        compiler_params=pltpu.CompilerParams(vmem_limit_bytes=VLIM),
        name="conv_norm_mlp",
    )(flags, x, hr, hc, mask, cot, depth_kernel.reshape(49, C), bias.reshape(1, C), gain.reshape(1, C),
      w_in, w_in.T, w_out, w_out.T)


def back_kernel(flags, back, hr, hc, xp, cot, taps1, out, gk, ext, fold, taps, perm, gks):
    i = pl.program_id(0)

    @pl.when(i == 0)
    def _():
        for t in range(49):
            taps[t] = jnp.broadcast_to(taps1[t:t + 1], (16, C))
        for t in range(49):
            taps[49 + t] = taps[48 - t]
        col = swap(iota2((1, COLS), 1))
        place_e = place(96, True)
        amat = one_hot(place_e == col)
        h = iota2((1, 32), 1)
        bmat = one_hot(place_e == jnp.where(h < 16, h - 16, 240 + h))
        perm[...] = one_hot(swap(iota2((COLS, 1), 0)) == iota2((1, COLS), 1))
        gks[...] = jnp.zeros_like(gks)

        def put(dst, e, main, rim):
            rim = rim.astype(bf16).reshape(6, 16, C)
            dst[e, 3:19] = main.reshape(16, 16, C)
            dst[e, 0:3] = rim[0:3]
            dst[e, 19:22] = rim[3:6]

        def inner(j, _):
            b0 = back[2 * j]
            b1 = back[2 * j + 1]
            main = jnp.concatenate([b0, b1], axis=-1)
            side = jnp.concatenate([hc[2 * j + 3], hc[2 * j + 4]], axis=-1)
            rim = dot(amat, main) + dot(bmat, side)
            put(ext, 2 * j + 3, b0, rim[:, :C])
            put(ext, 2 * j + 4, b1, rim[:, C:])
            return 0

        lax.fori_loop(0, ROWS // 2, inner, 0)
        is_bottom = flags[0] == 1
        is_top = flags[1] == 1
        zero_m = jnp.zeros((COLS, C), bf16)
        zero_s = jnp.zeros((32, C), bf16)
        for e in range(3):
            main = jnp.where(is_bottom, zero_m, hr[e])
            put(ext, e, main, dot(amat, main) + dot(bmat, jnp.where(is_bottom, zero_s, hc[e])))
            main = jnp.where(is_top, zero_m, hr[3 + e])
            put(ext, 35 + e, main, dot(amat, main) + dot(bmat, jnp.where(is_top, zero_s, hc[35 + e])))
        amat_f = one_hot(place(EXT, False) == 255 - col)
        bmat_f = one_hot(place_e == jnp.where(h < 16, -1 - h, 287 - h))
        for m in range(3):
            full = dot(amat_f, hr[5 - m])
            rim = dot(bmat_f, hc[37 - m])
            full = jnp.concatenate([full[:48] + rim[:48], full[48:304], full[304:] + rim[48:]], axis=0).astype(bf16)
            fold[m] = jnp.where(is_top, full, jnp.zeros_like(full)).reshape(22, 16, C)

    def add_row(src, pairs, r, k0, nk, acc, tap0):
        xv = [xp[r, (k0 + k) * 16:(k0 + k + 1) * 16] for k in range(nk)]
        for row, a in pairs:
            win = [src[row, k0 + kk] for kk in range(nk + 6)]
            w = [taps[tap0 + a * 7 + b] for b in range(7)]
            for k in range(nk):
                p = win[k] * w[0]
                for b in range(1, 7):
                    p = p + win[k + b] * w[b]
                p = p.astype(f32)
                acc[k] = p if acc[k] is None else acc[k] + p
            for b in range(7):
                q = win[b] * xv[0]
                for k in range(1, nk):
                    q = q + win[k + b] * xv[k]
                t = a * 7 + b
                q = q.astype(f32)
                gks[(48 - t) if tap0 else t] += q[:8] + q[8:]

    for r in range(RB):
        row = i * RB + r
        accs = []
        for k0 in (0, 8):
            acc = [None] * 8
            add_row(ext, [(row + a, a) for a in range(7)], r, k0, 8, acc, 49)
            accs += acc
        conv = jnp.concatenate(accs, axis=0)
        out[r] = (cot[r].astype(f32) + dot(perm[...], conv.astype(bf16))).astype(bf16)

    @pl.when((i == ROWS // RB - 1) & (flags[1] == 1))
    def _():
        for t in range(3):
            r = RB - 3 + t
            accs = []
            for k0 in (0, 8):
                acc = [None] * 8
                add_row(fold, [(m, 6 - t + m) for m in range(t + 1)], r, k0, 8, acc, 0)
                accs += acc
            conv = jnp.concatenate(accs, axis=0)
            out[r] = (out[r].astype(f32) + dot(perm[...], conv.astype(bf16))).astype(bf16)

    @pl.when(i == ROWS // RB - 1)
    def _():
        gk[...] = jnp.zeros_like(gk)
        for t in range(49):
            gk[t:t + 1] = jnp.sum(gks[t], axis=0, keepdims=True)


RB = 4


def back_call(flags, back, hr, hc, xp, cot, depth_kernel):
    vm = pl.BlockSpec(memory_space=pltpu.VMEM)
    blk = pl.BlockSpec((RB, COLS, C), lambda i: (i, 0, 0))
    return pl.pallas_call(
        back_kernel,
        grid=(ROWS // RB,),
        in_specs=[pl.BlockSpec(memory_space=pltpu.SMEM), vm, vm, vm, blk, blk, vm],
        out_specs=[blk, pl.BlockSpec((64, C), lambda i: (0, 0))],
        out_shape=[jax.ShapeDtypeStruct((ROWS, COLS, C), bf16), jax.ShapeDtypeStruct((64, C), f32)],
        scratch_shapes=[
            pltpu.VMEM((38, 22, 16, C), bf16), pltpu.VMEM((3, 22, 16, C), bf16), pltpu.VMEM((98, 16, C), bf16),
            pltpu.VMEM((COLS, COLS), bf16), pltpu.VMEM((49, 8, C), f32)],
        compiler_params=pltpu.CompilerParams(vmem_limit_bytes=VLIM),
        name="conv_back",
    )(flags, back, hr, hc, xp, cot, depth_kernel.reshape(49, C))


def neighbours(lat, lon):
    nl = lax.axis_size("lon")
    top = lat == lax.axis_size("lat") - 1
    low = lat > 0
    left = lax.rem(lon + nl - 1, nl)
    right = lax.rem(lon + 1, nl)
    up = jnp.where(top, lat, lat + 1)
    down = jnp.where(low, lat - 1, lat)
    f0 = jnp.where(top, nl - 1 - lon, lon)
    fl = jnp.where(top, lax.rem(nl - lon, nl), left)
    fr = jnp.where(top, lax.rem(2 * nl - 2 - lon, nl), right)
    return top, low, up, down, left, right, f0, fl, fr


def halo_kernel(rows, lcols, rcols, hr, hc, send, recv):
    lat = lax.axis_index("lat")
    lon = lax.axis_index("lon")
    top, low, up, down, left, right, f0, fl, fr = neighbours(lat, lon)
    far_l = jnp.logical_not(top & (fl == lon))
    far_r = jnp.logical_not(top & (fr == lon))
    inner = jnp.logical_not(top)

    def greet(a, b):
        pl.semaphore_signal(barrier, inc=1, device_id=(a, b), device_id_type=MESH)

    barrier = pltpu.get_barrier_semaphore()
    greet(lat, left)
    greet(lat, right)
    greet(up, f0)

    @pl.when(far_l)
    def _():
        greet(up, fl)

    @pl.when(far_r)
    def _():
        greet(up, fr)

    @pl.when(low)
    def _():
        greet(down, lon)
        greet(down, left)
        greet(down, right)

    count = 3 + jnp.where(far_l, 1, 0) + jnp.where(far_r, 1, 0) + jnp.where(low, 3, 0)
    pl.semaphore_wait(barrier, count)

    def copy(src, dst, s, slot, a, b):
        return pltpu.make_async_remote_copy(src_ref=src, dst_ref=dst, send_sem=send.at[s], recv_sem=recv.at[slot],
                                            device_id=(a, b), device_id_type=MESH)

    last = pl.ds(ROWS - 3, 3)
    first = pl.ds(0, 3)
    lo, mid, hi = pl.ds(0, 3), pl.ds(3, ROWS), pl.ds(ROWS + 3, 3)
    to_l, to_r = pl.ds(0, 16), pl.ds(16, 16)
    c_right = copy(rcols, hc.at[mid, to_l], 2, 2, lat, right)
    c_left = copy(lcols, hc.at[mid, to_r], 3, 3, lat, left)
    up_n = copy(rows.at[last], hr.at[pl.ds(0, 3)], 1, 0, up, f0)
    up_f = copy(rows.at[last], hr.at[pl.ds(3, 3)], 1, 1, up, f0)
    ul_n = copy(lcols.at[last], hc.at[lo, to_r], 6, 5, up, fl)
    ul_f = copy(lcols.at[last], hc.at[hi, to_l], 6, 6, up, fl)
    ur_n = copy(rcols.at[last], hc.at[lo, to_l], 7, 4, up, fr)
    ur_f = copy(rcols.at[last], hc.at[hi, to_r], 7, 7, up, fr)
    dn = copy(rows.at[first], hr.at[pl.ds(3, 3)], 0, 1, down, lon)
    dl = copy(lcols.at[first], hc.at[hi, to_r], 4, 7, down, left)
    dr = copy(rcols.at[first], hc.at[hi, to_l], 5, 6, down, right)
    own_l = pltpu.make_async_copy(lcols.at[last], hc.at[hi, to_l], send.at[6])
    own_r = pltpu.make_async_copy(rcols.at[last], hc.at[hi, to_r], send.at[7])

    @pl.when(inner)
    def _():
        up_n.start()
        ul_n.start()
        ur_n.start()

    @pl.when(top)
    def _():
        up_f.start()

    @pl.when(top & far_l)
    def _():
        ul_f.start()

    @pl.when(top & far_r)
    def _():
        ur_f.start()

    @pl.when(jnp.logical_not(far_l))
    def _():
        own_l.start()

    @pl.when(jnp.logical_not(far_r))
    def _():
        own_r.start()

    @pl.when(low)
    def _():
        dn.start()
        dl.start()
        dr.start()

    c_right.start()
    c_left.start()
    c_right.wait()
    c_left.wait()

    dn.wait_recv()

    @pl.when(far_l)
    def _():
        dr.wait_recv()

    @pl.when(far_r)
    def _():
        dl.wait_recv()

    @pl.when(jnp.logical_not(far_l))
    def _():
        own_l.wait()

    @pl.when(jnp.logical_not(far_r))
    def _():
        own_r.wait()

    @pl.when(low)
    def _():
        up_n.wait_recv()
        ul_n.wait_recv()
        ur_n.wait_recv()
        dn.wait_send()
        dl.wait_send()
        dr.wait_send()

    up_n.wait_send()

    @pl.when(far_l)
    def _():
        ul_n.wait_send()

    @pl.when(far_r)
    def _():
        ur_n.wait_send()


def halo_call(rows, lcols, rcols, ident):
    hbm = pl.BlockSpec(memory_space=pl.ANY)
    return pl.pallas_call(
        halo_kernel,
        in_specs=[hbm] * 3,
        out_specs=[hbm] * 2,
        out_shape=[jax.ShapeDtypeStruct((6, COLS, C), bf16), jax.ShapeDtypeStruct((ROWS + 6, 32, C), bf16)],
        scratch_shapes=[pltpu.SemaphoreType.DMA((8,)), pltpu.SemaphoreType.DMA((8,))],
        compiler_params=pltpu.CompilerParams(collective_id=ident, has_side_effects=True),
        name="halo",
    )(rows, lcols, rcols)


N_LON = 16
N_LAT = 8
SEG = 64


def sum_kernel(w, small, scale, out_w, out_s, wb, sb, r1, r2, r3, c2, s1, q1, s2, q2, s3, q3):
    lat = lax.axis_index("lat")
    lon = lax.axis_index("lon")
    barrier = pltpu.get_barrier_semaphore()

    def greet_lon(d, _):
        pl.semaphore_signal(barrier, inc=1, device_id=(lat, lax.rem(lon + d, N_LON)), device_id_type=MESH)
        return 0

    def greet_lat(d, _):
        pl.semaphore_signal(barrier, inc=1, device_id=(lax.rem(lat + d, N_LAT), lon), device_id_type=MESH)
        return 0

    lax.fori_loop(1, N_LON, greet_lon, 0)
    lax.fori_loop(1, N_LAT, greet_lat, 0)
    for c in range(N_LON):
        wb[c, 0:SEG] = w[c * SEG:(c + 1) * SEG].astype(bf16)
        wb[c, SEG:2 * SEG] = small[...].astype(bf16)
    pl.semaphore_wait(barrier, N_LON + N_LAT - 2)

    def first(d):
        to = lax.rem(lon + d, N_LON)
        return pltpu.make_async_remote_copy(src_ref=wb.at[to], dst_ref=r1.at[d], send_sem=s1.at[d], recv_sem=q1.at[d],
                                            device_id=(lat, to), device_id_type=MESH)

    def second(d):
        return pltpu.make_async_remote_copy(src_ref=c2, dst_ref=r2.at[lat], send_sem=s2.at[d], recv_sem=q2.at[d],
                                            device_id=(lax.rem(lat + d, N_LAT), lon), device_id_type=MESH)

    def third(d):
        return pltpu.make_async_remote_copy(src_ref=sb, dst_ref=r3.at[lon], send_sem=s3.at[d], recv_sem=q3.at[d],
                                            device_id=(lat, lax.rem(lon + d, N_LON)), device_id_type=MESH)

    def run(make, n):
        def go(d, _):
            make(d).start()
            return 0

        lax.fori_loop(1, n, go, 0)

    def arrive(make, n):
        def go(d, _):
            make(d).wait()
            return 0

        lax.fori_loop(1, n, go, 0)

    run(first, N_LON)
    arrive(first, N_LON)
    total = wb[lon].astype(f32)
    for d in range(1, N_LON):
        total = total + r1[d].astype(f32)
    c2[...] = total.astype(bf16)
    run(second, N_LAT)
    r2[lat] = c2[...]
    arrive(second, N_LAT)
    total = r2[0].astype(f32)
    for d in range(1, N_LAT):
        total = total + r2[d].astype(f32)
    total = total * scale[0]
    sb[...] = total[:SEG].astype(bf16)
    run(third, N_LON)
    out_s[...] = total[SEG:]
    r3[lon] = sb[...]
    arrive(third, N_LON)
    for c in range(N_LON):
        out_w[c * SEG:(c + 1) * SEG] = r3[c].astype(f32)


def sum_call(w, small, scale):
    vm = pl.BlockSpec(memory_space=pltpu.VMEM)
    dma = pltpu.SemaphoreType.DMA
    return pl.pallas_call(
        sum_kernel,
        in_specs=[vm, vm, pl.BlockSpec(memory_space=pltpu.SMEM)],
        out_specs=[vm, vm],
        out_shape=[jax.ShapeDtypeStruct((1024, C), f32), jax.ShapeDtypeStruct((SEG, C), f32)],
        scratch_shapes=[
            pltpu.VMEM((N_LON, 2 * SEG, C), bf16), pltpu.VMEM((SEG, C), bf16),
            pltpu.VMEM((N_LON, 2 * SEG, C), bf16), pltpu.VMEM((N_LAT, 2 * SEG, C), bf16), pltpu.VMEM((N_LON, SEG, C), bf16),
            pltpu.VMEM((2 * SEG, C), bf16),
            dma((N_LON,)), dma((N_LON,)), dma((N_LAT,)), dma((N_LAT,)), dma((N_LON,)), dma((N_LON,))],
        compiler_params=pltpu.CompilerParams(collective_id=2, has_side_effects=True, vmem_limit_bytes=VLIM),
        name="sum_grads",
    )(w, small, scale)


def body(ocean_state, sea_mask, depth_kernel, conv_bias, norm_gain, w_in, w_out, cotangent):
    lat = lax.axis_index("lat")
    flags = jnp.stack([lat == 0, lat == lax.axis_size("lat") - 1]).astype(jnp.int32)
    hr, hc = halo_call(ocean_state, ocean_state[:, :16], ocean_state[:, COLS - 16:], 0)
    upd, back, edge, xp, gin, gout, small = main_call(
        flags, ocean_state, hr, hc, sea_mask, cotangent, depth_kernel, conv_bias, norm_gain, w_in, w_out)
    hr2, hc2 = halo_call(back, edge[:, :16], edge[:, 16:], 1)
    grad_state, gk = back_call(flags, back, hr2, hc2, xp, cotangent, depth_kernel)
    cells = COLS * ROWS * lax.axis_size("lat") * lax.axis_size("lon")
    scale = 1.0 / jnp.sqrt(jnp.full((1,), cells, f32))
    extra = jnp.concatenate([gk[:49], jnp.sum(small[:8], axis=0, keepdims=True),
                             jnp.sum(small[8:], axis=0, keepdims=True), jnp.zeros((13, C), f32)], axis=0)
    w = jnp.concatenate([gin.reshape(512, C), gout.reshape(512, C)], axis=0)
    out_w, out_s = sum_call(w, extra, scale)
    return (upd, grad_state, out_s[:49].reshape(7, 7, C), out_s[50], out_s[49],
            out_w[:512].reshape(C, HID), out_w[512:].reshape(C, HID).T)


def solution(mesh):
    tile = P("lat", "lon", None)
    return jax.shard_map(
        body,
        mesh=mesh,
        in_specs=(tile, P("lat", "lon"), P(), P(), P(), P(), P(), tile),
        out_specs=(tile, tile, P(), P(), P(), P(), P()),
        check_vma=False,
    )
```

time: 434 us -> 180 us (0.41)
  Pallas kernels: 0 us -> 162 us
  other arithmetic: 147 us -> 2.86 us
  waiting for transfers between devices: 102 us -> 0 us
  blocking collectives: 67.8 us -> 0 us
  matrix products: 54.4 us -> 0 us
  starting transfers between devices: 33 us -> 0 us
  between operations: 15.6 us -> 0.71 us
    pallas_call x0 -> x5, Pallas kernels: none -> 162 us  [the longest x1 53 us: main_call(): pl.pallas_call(main_kernel, grid=(NB + 1,), in_specs=[pl.BlockSpec(memory...]
    psum x1 -> x0, waiting for transfers between devices: 79.3 us -> none  [body(): lax.psum((kernel_grad, bias_grad, gain_part, in_part, out_part), ('lat',...]
    psum x1 -> x0, blocking collectives: 67.8 us -> none  [body(): lax.psum((kernel_grad, bias_grad, gain_part, in_part, out_part), ('lat',...]
    reduce_sum x5 -> x1, other arithmetic: 67.9 us -> 0.73 us  [body(): jnp.sum(small[:8], axis=0, keepdims=True)]
    dot_general x6 -> x0, matrix products: 54.4 us -> none  [the longest x1 19.4 us: column_mlp(): jnp.dot(hidden, w_out, preferred_element_type=jnp.float32)]
    add x3 -> x0, other arithmetic: 51.8 us -> none  [the longest x1 48.6 us: body(): state_grad = cotangent.astype(jnp.float32) + inner_grad]
    ppermute x16 -> x0, starting transfers between devices: 33 us -> none  [the longest x4 17 us: with_halo(): lax.ppermute(lax.slice_in_dim(block, block.shape[dim] - width, None, axis...]
    ppermute x16 -> x0, waiting for transfers between devices: 22.2 us -> none  [the longest x8 17.7 us: partner(): return lax.ppermute(value, axis, pairs)]
  transfers between devices with their start and end apart: 17 -> 0, of which waited for: 9 -> 0; matrix products, arithmetic and copies ran while one was open for 17% -> 0% of each run, Pallas kernels for 0% -> 0%
where the time goes in v1:
time: 180 us; the launch traced here: 179 us
  Pallas kernels  162 us (90%)
  local copies, waits for them, and re-layouts  13.6 us (8%)
  other arithmetic  2.86 us (2%)
    pallas_call x1, Pallas kernels, main_call(): pl.pallas_call(main_kernel, grid=(NB + 1,), in_specs=[pl.BlockSpec(memory...  53 us
    pallas_call x1, Pallas kernels, back_call(): pl.pallas_call(back_kernel, grid=(ROWS // RB,), in_specs=[pl.BlockSpec(me...  37.4 us
    pallas_call x1, Pallas kernels, sum_call(): pl.pallas_call(sum_kernel, in_specs=[vm, vm, pl.BlockSpec(memory_space=pl...  36.9 us
    pallas_call x2, Pallas kernels, halo_call(): pl.pallas_call(halo_kernel, in_specs=[hbm] * 3, out_specs=[hbm] * 2, out_...  35 us

profile of v1, /device:TPU:1, one launch (start us, length us, event | category | flops | bytes accessed | tf_op | source)
XLA Modules:
  0.0 179.5 jit_solution(14883398031983141906)
XLA Ops:
  0.6 0.6 add_convert_fusion.flags
  1.2 0.1 pad.3.clone
  1.3 1.3 reshape.39.taps1
  2.6 1.7 copy.15
  4.3 1.6 copy.16
  5.9 1.7 fusion
  7.6 19.1 %halo.2 = (bf16[6,256,128]{2,1,0:T(8,128)(2,1)}, bf16[38,32,128]{2,1,0:T(8,128)(2,1)}) custom-call(bf16[32,256,128]{2,1,0:T(8,128)(2,1)} %x.1, bf16[32,16,128]{2,1,0:T(8,128)(2,1)} %get-tuple-element.40.lcols, bf16[32,16,128]{2,1,0:T(8,128)(2,1)} %get-tuple-element.39.rcols), custom_call_target="tpu_custom_call" | custom-call | tf_op jit(solution)/shard_map/halo/pallas_call | solution.py:485
  26.7 53.0 %conv_norm_mlp.1 = (bf16[32,256,128]{2,1,0:T(8,128)(2,1)}, bf16[32,256,128]{2,1,0:T(8,128)(2,1)}, bf16[32,32,128]{2,1,0:T(8,128)(2,1)}, bf16[32,256,128]{2,1,0:T...) custom-call(s32[2]{0:T(128)} %add_convert_fusion.flags, bf16[32,256,128]{2,1,0:T(8,128)(2,1)} %x.1, ...), custom_call_target="tpu_custom_call" | custom-call | tf_op jit(solution)/shard_map/conv_norm_mlp/pallas_call | solution.py:199
  79.7 0.0 copy-start
  79.7 0.7 slice_reduce_fusion.1
  80.5 1.0 reshape.42
  81.4 1.0 reshape.43
  82.4 0.8 pad_maximum_fusion.w
  83.2 0.0 copy-done
  83.2 0.7 fusion.2
  84.0 15.9 %halo.3 = (bf16[6,256,128]{2,1,0:T(8,128)(2,1)}, bf16[38,32,128]{2,1,0:T(8,128)(2,1)}) custom-call(bf16[32,256,128]{2,1,0:T(8,128)(2,1)} %get-tuple-element.25.rows.back, bf16[32,16,128]{2,1,0:T(8,128)(2,1)} %get-tuple-element.44.lcols, bf16[32,16,128]{2,1,0:T(8,128)(2,1)} %get-tuple-element.43.rcols), custom_call_target="tpu_custom_call" | custom-call | tf_op jit(solution)/shard_map/halo/pallas_call | solution.py:485
  99.9 37.4 %conv_back.1 = (bf16[32,256,128]{2,1,0:T(8,128)(2,1)}, f32[64,128]{1,0:T(8,128)}) custom-call(s32[2]{0:T(128)} %add_convert_fusion.flags, bf16[32,256,128]{2,1,0:T(8,128)(2,1)} %get-tuple-element.25.rows.back, bf16[6,256,128]{2,1,0:T(8,128)(2,1)} %get-tuple-element.27.hr, bf16[38,32,128]{2,1,0:T(8,128)(2,1)} %get-tuple-element.28.hc, ...), custom_call_target="tpu_custom_call" | custom-call | tf_op jit(solution)/shard_map/conv_back/pallas_call | solution.py:325
  137.2 0.8 slice.40
  138.0 0.7 maximum_maximum_fusion.small
  138.7 36.9 %sum_grads.1 = (f32[1024,128]{1,0:T(8,128)}, f32[64,128]{1,0:T(8,128)}) custom-call(f32[1024,128]{1,0:T(8,128)} %pad_maximum_fusion.w, f32[64,128]{1,0:T(8,128)} %maximum_maximum_fusion.small, f32[1]{0:T(128)} %constant.14.clone.1.scale), custom_call_target="tpu_custom_call" | custom-call | tf_op jit(solution)/shard_map/sum_grads/pallas_call | solution.py:573
  175.6 0.0 copy-start.1
  175.6 1.1 fusion.1
  176.7 0.8 copy.17
  177.6 0.0 copy-done.1
  177.6 0.5 slice_bitcast_fusion
  178.1 0.6 reshape.44
  178.7 0.7 reshape.45
  (3 shorter events, 0.0 us)
Async XLA Ops:
  79.7 3.5 %copy-start = (bf16[32,32,128]{2,1,0:T(8,128)(2,1)S(1)}, bf16[32,32,128]{2,1,0:T(8,128)(2,1)}, u32[]{:S(2)}) copy-start(bf16[32,32,128]{2,1,0:T(8,128)(2,1)} %get-tuple-element.26) | copy-start | bytes 786436
  175.6 2.0 %copy-start.1 = (f32[64,128]{1,0:T(8,128)S(1)}, f32[64,128]{1,0:T(8,128)}, u32[]{:S(2)}) copy-start(f32[64,128]{1,0:T(8,128)} %get-tuple-element.35) | copy-start | bytes 98308

commit v2 on v1

--- a/solution.py
+++ b/solution.py
@@ -76,15 +76,16 @@
 NB = ROWS // R
 
 
-def main_kernel(flags, x, hr, hc, mask, cot, taps1, bias, gain, w_in, w_in_t, w_out, w_out_t,
+def main_kernel(x, mask, cot, taps1, bias, gain, w_in, w_in_t, w_out, w_out_t,
                 upd, back, edge, xp, gin, gout, small,
-                ext, taps, perm, norm_s, unit_s, inv_s, up_s, mask_s, xs_s):
+                ext, taps, perm, norm_s, unit_s, inv_s, up_s, mask_s, xs_s, hr, hc, send, recv):
     i = pl.program_id(0)
 
     @pl.when(i == 0)
     def _():
+        exchange(x, x.at[:, pl.ds(0, 16)], x.at[:, pl.ds(COLS - 16, 16)], hr, hc, send, recv)
         for t in range(49):
-            taps[t] = jnp.broadcast_to(taps1[t:t + 1], (16, C))
+            taps[t] = jnp.broadcast_to(taps1[t // 7, t % 7:t % 7 + 1], (16, C))
         col = iota2((1, COLS), 1)
         amat = one_hot(place(EXT, False) == col)
         h = iota2((1, 32), 1)
@@ -105,8 +106,8 @@
             return 0
 
         lax.fori_loop(0, ROWS // 2, inner, 0)
-        is_bottom = flags[0] == 1
-        is_top = flags[1] == 1
+        is_bottom = lax.axis_index("lat") == 0
+        is_top = lax.axis_index("lat") == lax.axis_size("lat") - 1
         for e in range(3):
             main = jnp.where(is_bottom, jnp.zeros((COLS, C), bf16), hr[e])
             side = jnp.where(is_bottom, jnp.zeros((32, C), bf16), hc[e])
@@ -190,7 +191,7 @@
         xp[r] = ext[row + 3, 3:19].reshape(COLS, C)
 
 
-def main_call(flags, x, hr, hc, mask, cot, depth_kernel, bias, gain, w_in, w_out):
+def main_call(x, mask, cot, depth_kernel, bias, gain, w_in, w_out):
     vm = pl.BlockSpec(memory_space=pltpu.VMEM)
     now = lambda i: (jnp.minimum(i, NB - 1), 0, 0)
     past = lambda i: (jnp.maximum(i - 1, 0), 0, 0)
@@ -199,8 +200,7 @@
     return pl.pallas_call(
         main_kernel,
         grid=(NB + 1,),
-        in_specs=[pl.BlockSpec(memory_space=pltpu.SMEM), vm, vm, vm, vm,
-                  pl.BlockSpec((R, COLS, C), now), vm, vm, vm, vm, vm, vm, vm],
+        in_specs=[vm, vm, pl.BlockSpec((R, COLS, C), now), vm, vm, vm, vm, vm, vm, vm],
         out_specs=[pl.BlockSpec((R, COLS, C), past), pl.BlockSpec((R, COLS, C), past),
                    pl.BlockSpec((R, 32, C), past), pl.BlockSpec((R, COLS, C), now),
                    pl.BlockSpec((C, HID), whole2), pl.BlockSpec((C, HID), whole2), pl.BlockSpec((16, C), whole2)],
@@ -210,20 +210,23 @@
         scratch_shapes=[
             pltpu.VMEM((38, 22, 16, C), bf16), pltpu.VMEM((49, 16, C), bf16), pltpu.VMEM((COLS, COLS), bf16),
             pltpu.VMEM((2, M, C), bf16), pltpu.VMEM((2, M, C), f32), pltpu.VMEM((2, M, C), f32),
-            pltpu.VMEM((2, M, C), bf16), pltpu.VMEM((2, M, C), f32), pltpu.VMEM((2, M, C), bf16)],
-        compiler_params=pltpu.CompilerParams(vmem_limit_bytes=VLIM),
+            pltpu.VMEM((2, M, C), bf16), pltpu.VMEM((2, M, C), f32), pltpu.VMEM((2, M, C), bf16),
+            pltpu.VMEM((6, COLS, C), bf16), pltpu.VMEM((ROWS + 6, 32, C), bf16),
+            pltpu.SemaphoreType.DMA((8,)), pltpu.SemaphoreType.DMA((8,))],
+        compiler_params=pltpu.CompilerParams(collective_id=0, has_side_effects=True, vmem_limit_bytes=VLIM),
         name="conv_norm_mlp",
-    )(flags, x, hr, hc, mask, cot, depth_kernel.reshape(49, C), bias.reshape(1, C), gain.reshape(1, C),
+    )(x, mask, cot, depth_kernel, bias.reshape(1, C), gain.reshape(1, C),
       w_in, w_in.T, w_out, w_out.T)
 
 
-def back_kernel(flags, back, hr, hc, xp, cot, taps1, out, gk, ext, fold, taps, perm, gks):
+def back_kernel(back, edge, xp, cot, taps1, out, gk, ext, fold, taps, perm, gks, hr, hc, send, recv):
     i = pl.program_id(0)
 
     @pl.when(i == 0)
     def _():
+        exchange(back, edge.at[:, pl.ds(0, 16)], edge.at[:, pl.ds(16, 16)], hr, hc, send, recv)
         for t in range(49):
-            taps[t] = jnp.broadcast_to(taps1[t:t + 1], (16, C))
+            taps[t] = jnp.broadcast_to(taps1[t // 7, t % 7:t % 7 + 1], (16, C))
         for t in range(49):
             taps[49 + t] = taps[48 - t]
         col = swap(iota2((1, COLS), 1))
@@ -251,8 +254,8 @@
             return 0
 
         lax.fori_loop(0, ROWS // 2, inner, 0)
-        is_bottom = flags[0] == 1
-        is_top = flags[1] == 1
+        is_bottom = lax.axis_index("lat") == 0
+        is_top = lax.axis_index("lat") == lax.axis_size("lat") - 1
         zero_m = jnp.zeros((COLS, C), bf16)
         zero_s = jnp.zeros((32, C), bf16)
         for e in range(3):
@@ -297,7 +300,7 @@
         conv = jnp.concatenate(accs, axis=0)
         out[r] = (cot[r].astype(f32) + dot(perm[...], conv.astype(bf16))).astype(bf16)
 
-    @pl.when((i == ROWS // RB - 1) & (flags[1] == 1))
+    @pl.when((i == ROWS // RB - 1) & (lax.axis_index("lat") == lax.axis_size("lat") - 1))
     def _():
         for t in range(3):
             r = RB - 3 + t
@@ -319,21 +322,23 @@
 RB = 4
 
 
-def back_call(flags, back, hr, hc, xp, cot, depth_kernel):
+def back_call(back, edge, xp, cot, depth_kernel):
     vm = pl.BlockSpec(memory_space=pltpu.VMEM)
     blk = pl.BlockSpec((RB, COLS, C), lambda i: (i, 0, 0))
     return pl.pallas_call(
         back_kernel,
         grid=(ROWS // RB,),
-        in_specs=[pl.BlockSpec(memory_space=pltpu.SMEM), vm, vm, vm, blk, blk, vm],
+        in_specs=[vm, vm, blk, blk, vm],
         out_specs=[blk, pl.BlockSpec((64, C), lambda i: (0, 0))],
         out_shape=[jax.ShapeDtypeStruct((ROWS, COLS, C), bf16), jax.ShapeDtypeStruct((64, C), f32)],
         scratch_shapes=[
             pltpu.VMEM((38, 22, 16, C), bf16), pltpu.VMEM((3, 22, 16, C), bf16), pltpu.VMEM((98, 16, C), bf16),
-            pltpu.VMEM((COLS, COLS), bf16), pltpu.VMEM((49, 8, C), f32)],
-        compiler_params=pltpu.CompilerParams(vmem_limit_bytes=VLIM),
+            pltpu.VMEM((COLS, COLS), bf16), pltpu.VMEM((49, 8, C), f32),
+            pltpu.VMEM((6, COLS, C), bf16), pltpu.VMEM((ROWS + 6, 32, C), bf16),
+            pltpu.SemaphoreType.DMA((8,)), pltpu.SemaphoreType.DMA((8,))],
+        compiler_params=pltpu.CompilerParams(collective_id=1, has_side_effects=True, vmem_limit_bytes=VLIM),
         name="conv_back",
-    )(flags, back, hr, hc, xp, cot, depth_kernel.reshape(49, C))
+    )(back, edge, xp, cot, depth_kernel)
 
 
 def neighbours(lat, lon):
@@ -350,7 +355,7 @@
     return top, low, up, down, left, right, f0, fl, fr
 
 
-def halo_kernel(rows, lcols, rcols, hr, hc, send, recv):
+def exchange(rows, lcols, rcols, hr, hc, send, recv):
     lat = lax.axis_index("lat")
     lon = lax.axis_index("lon")
     top, low, up, down, left, right, f0, fl, fr = neighbours(lat, lon)
@@ -480,25 +485,12 @@
         ur_n.wait_send()
 
 
-def halo_call(rows, lcols, rcols, ident):
-    hbm = pl.BlockSpec(memory_space=pl.ANY)
-    return pl.pallas_call(
-        halo_kernel,
-        in_specs=[hbm] * 3,
-        out_specs=[hbm] * 2,
-        out_shape=[jax.ShapeDtypeStruct((6, COLS, C), bf16), jax.ShapeDtypeStruct((ROWS + 6, 32, C), bf16)],
-        scratch_shapes=[pltpu.SemaphoreType.DMA((8,)), pltpu.SemaphoreType.DMA((8,))],
-        compiler_params=pltpu.CompilerParams(collective_id=ident, has_side_effects=True),
-        name="halo",
-    )(rows, lcols, rcols)
-
-
 N_LON = 16
 N_LAT = 8
 SEG = 64
 
 
-def sum_kernel(w, small, scale, out_w, out_s, wb, sb, r1, r2, r3, c2, s1, q1, s2, q2, s3, q3):
+def sum_kernel(gin, gout, gk, small, scale, o_in, o_out, o_k, o_bias, o_gain, wb, sb, r1, r2, r3, c2, s1, q1, s2, q2, s3, q3):
     lat = lax.axis_index("lat")
     lon = lax.axis_index("lon")
     barrier = pltpu.get_barrier_semaphore()
@@ -513,9 +505,13 @@
 
     lax.fori_loop(1, N_LON, greet_lon, 0)
     lax.fori_loop(1, N_LAT, greet_lat, 0)
+    rest = jnp.concatenate([gk[:49], jnp.sum(small[:8], axis=0, keepdims=True),
+                            jnp.sum(small[8:], axis=0, keepdims=True), jnp.zeros((13, C), f32)], axis=0).astype(bf16)
     for c in range(N_LON):
-        wb[c, 0:SEG] = w[c * SEG:(c + 1) * SEG].astype(bf16)
-        wb[c, SEG:2 * SEG] = small[...].astype(bf16)
+        r0, c0 = c // 4 * 32, c % 4 * C
+        wb[c, 0:32] = gin[r0:r0 + 32, c0:c0 + C].astype(bf16)
+        wb[c, 32:SEG] = gout[r0:r0 + 32, c0:c0 + C].astype(bf16)
+        wb[c, SEG:2 * SEG] = rest
     pl.semaphore_wait(barrier, N_LON + N_LAT - 2)
 
     def first(d):
@@ -560,21 +556,28 @@
     total = total * scale[0]
     sb[...] = total[:SEG].astype(bf16)
     run(third, N_LON)
-    out_s[...] = total[SEG:]
+    for a in range(7):
+        o_k[a] = total[SEG + 7 * a:SEG + 7 * a + 7]
+    o_gain[...] = total[SEG + 49:SEG + 50]
+    o_bias[...] = total[SEG + 50:SEG + 51]
     r3[lon] = sb[...]
     arrive(third, N_LON)
-    for c in range(N_LON):
-        out_w[c * SEG:(c + 1) * SEG] = r3[c].astype(f32)
-
-
-def sum_call(w, small, scale):
+    for j in range(4):
+        for k in range(4):
+            o_in[32 * k:32 * k + 32, j * C:(j + 1) * C] = r3[4 * k + j, 0:32].astype(f32)
+        whole = jnp.concatenate([r3[4 * k + j, 32:SEG] for k in range(4)], axis=0).astype(f32)
+        o_out[j * C:(j + 1) * C] = whole.T
+
+
+def sum_call(gin, gout, gk, small, scale):
     vm = pl.BlockSpec(memory_space=pltpu.VMEM)
     dma = pltpu.SemaphoreType.DMA
     return pl.pallas_call(
         sum_kernel,
-        in_specs=[vm, vm, pl.BlockSpec(memory_space=pltpu.SMEM)],
-        out_specs=[vm, vm],
-        out_shape=[jax.ShapeDtypeStruct((1024, C), f32), jax.ShapeDtypeStruct((SEG, C), f32)],
+        in_specs=[vm, vm, vm, vm, pl.BlockSpec(memory_space=pltpu.SMEM)],
+        out_specs=[vm] * 5,
+        out_shape=[jax.ShapeDtypeStruct((C, HID), f32), jax.ShapeDtypeStruct((HID, C), f32),
+                   jax.ShapeDtypeStruct((7, 7, C), f32), jax.ShapeDtypeStruct((1, C), f32), jax.ShapeDtypeStruct((1, C), f32)],
         scratch_shapes=[
             pltpu.VMEM((N_LON, 2 * SEG, C), bf16), pltpu.VMEM((SEG, C), bf16),
             pltpu.VMEM((N_LON, 2 * SEG, C), bf16), pltpu.VMEM((N_LAT, 2 * SEG, C), bf16), pltpu.VMEM((N_LON, SEG, C), bf16),
@@ -582,25 +585,17 @@
             dma((N_LON,)), dma((N_LON,)), dma((N_LAT,)), dma((N_LAT,)), dma((N_LON,)), dma((N_LON,))],
         compiler_params=pltpu.CompilerParams(collective_id=2, has_side_effects=True, vmem_limit_bytes=VLIM),
         name="sum_grads",
-    )(w, small, scale)
+    )(gin, gout, gk, small, scale)
 
 
 def body(ocean_state, sea_mask, depth_kernel, conv_bias, norm_gain, w_in, w_out, cotangent):
-    lat = lax.axis_index("lat")
-    flags = jnp.stack([lat == 0, lat == lax.axis_size("lat") - 1]).astype(jnp.int32)
-    hr, hc = halo_call(ocean_state, ocean_state[:, :16], ocean_state[:, COLS - 16:], 0)
     upd, back, edge, xp, gin, gout, small = main_call(
-        flags, ocean_state, hr, hc, sea_mask, cotangent, depth_kernel, conv_bias, norm_gain, w_in, w_out)
-    hr2, hc2 = halo_call(back, edge[:, :16], edge[:, 16:], 1)
-    grad_state, gk = back_call(flags, back, hr2, hc2, xp, cotangent, depth_kernel)
+        ocean_state, sea_mask, cotangent, depth_kernel, conv_bias, norm_gain, w_in, w_out)
+    grad_state, gk = back_call(back, edge, xp, cotangent, depth_kernel)
     cells = COLS * ROWS * lax.axis_size("lat") * lax.axis_size("lon")
     scale = 1.0 / jnp.sqrt(jnp.full((1,), cells, f32))
-    extra = jnp.concatenate([gk[:49], jnp.sum(small[:8], axis=0, keepdims=True),
-                             jnp.sum(small[8:], axis=0, keepdims=True), jnp.zeros((13, C), f32)], axis=0)
-    w = jnp.concatenate([gin.reshape(512, C), gout.reshape(512, C)], axis=0)
-    out_w, out_s = sum_call(w, extra, scale)
-    return (upd, grad_state, out_s[:49].reshape(7, 7, C), out_s[50], out_s[49],
-            out_w[:512].reshape(C, HID), out_w[512:].reshape(C, HID).T)
+    o_in, o_out, o_k, o_bias, o_gain = sum_call(gin, gout, gk, small, scale)
+    return upd, grad_state, o_k, o_bias.reshape(C), o_gain.reshape(C), o_in, o_out
 
 
 def solution(mesh):

time: 180 us -> 173 us (0.961)
  local copies, waits for them, and re-layouts: 13.6 us -> 10.1 us
  other arithmetic: 2.86 us -> 0 us
    unnamed x6 -> x23, local copies, waits for them, and re-layouts: 3.31 us -> 10.1 us
    reshape x7 -> x0, local copies, waits for them, and re-layouts: 5.5 us -> none  [the longest x2 1.94 us: body(): w = jnp.concatenate([gin.reshape(512, C), gout.reshape(512, C)], axis=0)]
    slice x5 -> x0, local copies, waits for them, and re-layouts: 4.23 us -> none  [the longest x1 1.69 us: body(): ocean_state[:, COLS - 16:]]
    pallas_call x5 -> x3, Pallas kernels: 162 us -> 162 us  [the longest x1 71.6 us: main_call(): pl.pallas_call(main_kernel, grid=(NB + 1,), in_specs=[vm, vm, pl.BlockSpe...]
where the time goes in v2:
time: 173 us
  Pallas kernels  162 us (94%)
  local copies, waits for them, and re-layouts  10.1 us (6%)
    pallas_call x1, Pallas kernels, main_call(): pl.pallas_call(main_kernel, grid=(NB + 1,), in_specs=[vm, vm, pl.BlockSpe...  71.6 us
    pallas_call x1, Pallas kernels, back_call(): pl.pallas_call(back_kernel, grid=(ROWS // RB,), in_specs=[vm, vm, blk, bl...  53.4 us
    pallas_call x1, Pallas kernels, sum_call(): pl.pallas_call(sum_kernel, in_specs=[vm, vm, vm, vm, pl.BlockSpec(memory_...  37 us
    unnamed x23, local copies, waits for them, and re-layouts  10.1 us

profile of v2, /device:TPU:1, one launch (start us, length us, event | category | flops | bytes accessed | tf_op | source)
XLA Modules:
  0.0 172.7 jit_solution(15577321184514773551)
XLA Ops:
  0.6 1.7 copy.15
  2.3 1.7 copy.16
  4.0 71.6 %conv_norm_mlp.1 = (bf16[32,256,128]{2,1,0:T(8,128)(2,1)}, bf16[32,256,128]{2,1,0:T(8,128)(2,1)}, bf16[32,32,128]{2,1,0:T(8,128)(2,1)}, bf16[32,256,128]{2,1,0:T...) custom-call(bf16[32,256,128]{2,1,0:T(8,128)(2,1)} %x.1, s32[32,256]{1,0:T(8,128)} %mask.1, ...), custom_call_target="tpu_custom_call" | custom-call | tf_op jit(solution)/shard_map/conv_norm_mlp/pallas_call | solution.py:200
  75.5 0.0 copy-start
  75.5 53.4 %conv_back.1 = (bf16[32,256,128]{2,1,0:T(8,128)(2,1)}, f32[64,128]{1,0:T(8,128)}) custom-call(bf16[32,256,128]{2,1,0:T(8,128)(2,1)} %get-tuple-element.22.back, bf16[32,32,128]{2,1,0:T(8,128)(2,1)} %get-tuple-element.23.edge, bf16[32,256,128]{2,1,0:T(8,128)(2,1)} %get-tuple-element.24.xp, bf16[32,256,128]{2,1,0:T(8,128)(2,1)} %cot.3, bf16[7,7,128]{2,1,0:T(8,128)(2,1)} %taps1.3), custom_call_target="tpu_custom_call" | custom-call | tf_op jit(solution)/shard_map/conv_back/pallas_call | solution.py:328
  128.9 37.0 %sum_grads.1 = (f32[128,512]{1,0:T(8,128)}, f32[512,128]{1,0:T(8,128)}, f32[7,7,128]{2,1,0:T(8,128)}, f32[1,128]{1,0:T(1,128)}, f32[1,128]{1,0:T(1,128)}) custom-call(f32[128,512]{1,0:T(8,128)} %get-tuple-element.26.gin, f32[128,512]{1,0:T(8,128)} %get-tuple-element.27.gout, f32[64,128]{1,0:T(8,128)} %get-tuple-element.28.gk, ...), custom_call_target="tpu_custom_call" | custom-call | tf_op jit(solution)/shard_map/sum_grads/pallas_call | solution.py:575
  165.9 0.0 copy-done
  165.9 0.0 copy-start.1
  165.9 1.3 copy.24
  167.2 1.0 copy-done.1
  168.3 0.0 copy-start.4
  168.3 0.0 copy-start.6
  168.3 0.0 copy-start.5
  168.3 0.0 copy-start.3
  168.3 0.0 copy-start.2
  168.3 1.3 copy.25
  169.6 0.0 copy-done.4
  169.6 0.6 copy.26
  170.2 0.0 copy-done.6
  170.2 0.5 copy.27
  170.7 0.0 copy-done.5
  170.7 0.5 copy.28
  171.3 0.0 copy-done.3
  171.3 0.7 copy.29
  172.0 0.0 copy-done.2
  172.0 0.7 copy.30
Async XLA Ops:
  75.5 90.4 %copy-start = (bf16[32,256,128]{2,1,0:T(8,128)(2,1)S(1)}, bf16[32,256,128]{2,1,0:T(8,128)(2,1)}, u32[]{:S(2)}) copy-start(bf16[32,256,128]{2,1,0:T(8,128)(2,1)} %get-tuple-element.42) | copy-start | bytes 6291460
  165.9 2.3 %copy-start.1 = (bf16[32,256,128]{2,1,0:T(8,128)(2,1)S(1)}, bf16[32,256,128]{2,1,0:T(8,128)(2,1)}, u32[]{:S(2)}) copy-start(bf16[32,256,128]{2,1,0:T(8,128)(2,1)} %get-tuple-element.43) | copy-start | bytes 6291460
  168.3 1.3 copy-start.4
  168.3 2.0 %copy-start.6 = (f32[1,128]{1,0:T(1,128)S(1)}, f32[1,128]{1,0:T(1,128)}, u32[]{:S(2)}) copy-start(f32[1,128]{1,0:T(1,128)} %get-tuple-element.31) | copy-start | bytes 1540
  168.3 2.5 %copy-start.5 = (f32[1,128]{1,0:T(1,128)S(1)}, f32[1,128]{1,0:T(1,128)}, u32[]{:S(2)}) copy-start(f32[1,128]{1,0:T(1,128)} %get-tuple-element.32) | copy-start | bytes 1540
  168.3 3.0 %copy-start.3 = (f32[128,512]{1,0:T(8,128)S(1)}, f32[128,512]{1,0:T(8,128)}, u32[]{:S(2)}) copy-start(f32[128,512]{1,0:T(8,128)} %get-tuple-element.47) | copy-start | bytes 786436
  168.3 3.7 %copy-start.2 = (f32[512,128]{1,0:T(8,128)S(1)}, f32[512,128]{1,0:T(8,128)}, u32[]{:S(2)}) copy-start(f32[512,128]{1,0:T(8,128)} %get-tuple-element.48) | copy-start | bytes 786436

commit v3 on v0

v3 whole, which is shorter than its diff:
```python
import functools
import jax
import jax.numpy as jnp
from jax import lax
from jax.experimental import pallas as pl
from jax.experimental.pallas import tpu as pltpu
from jax.sharding import PartitionSpec as P

MESH = pl.DeviceIdType.MESH
bf16 = jnp.bfloat16
f32 = jnp.float32
epsilon = 1e-06
root_half = 0.7978845608028654
cubic_coef = 0.044715

C = 128
ROWS = 32
COLS = 256
HID = 512
EXT = 22 * 16
N_LON = 16
N_LAT = 8
SEG = 64
R = 2
M = R * COLS
NB = ROWS // R
FIRST = 7
CHUNKS = (3, 3, 4, 4, 5, 5)
VLIM = 60 * 1024 * 1024


def iota2(shape, dim):
    return lax.broadcasted_iota(jnp.int32, shape, dim)


def one_hot(hit):
    return jnp.where(hit, 1.0, 0.0).astype(bf16)


def swap(o):
    return (o % 16) * 16 + o // 16


def rim_place():
    o = iota2((96, 1), 0)
    o = jnp.where(o >= 48, o + 256, o)
    return (o % 16) * 16 + o // 16 - 3


def dot(a, b):
    return jnp.dot(a, b, preferred_element_type=f32)


def dot_t(a, b):
    return lax.dot_general(a, b, (((0,), (0,)), ((), ())), preferred_element_type=f32)


def conv_part(ext, row, wmat, flip, lo, hi):
    parts = []
    for u in range(lo, hi):
        j, b = u // 7, u % 7
        e = row + 2 * (3 - j if flip else j)
        s = 6 - b if flip else b
        pair = [ext[e, s:s + 16].reshape(COLS, C), ext[e + 1, s:s + 16].reshape(COLS, C)]
        parts += pair[::-1] if flip else pair
    return dot(jnp.concatenate(parts, axis=-1), wmat[lo * 256:hi * 256])


def gelu_parts(v):
    u = v * v
    t = jnp.tanh(v * (root_half + (root_half * cubic_coef) * u))
    h = 0.5 * t + 0.5
    act = v * h
    der = h + act * (1.0 - h) * (2.0 * root_half + (6.0 * root_half * cubic_coef) * u)
    return act, der


def main_block(n):
    late = n - FIRST
    edge = jnp.where(late < 2, late, late + 12)
    return jnp.where(n < FIRST, n + 2, jnp.where(late < 4, edge, n - 2))


def back_block(n):
    late = n - 12
    return jnp.where(n < 12, n + 2, jnp.where(late < 2, late, late + 12))


class Links:
    def __init__(self):
        self.lat = lax.axis_index("lat")
        self.lon = lax.axis_index("lon")
        lat, lon = self.lat, self.lon
        self.top = lat == N_LAT - 1
        self.low = lat > 0
        self.inner = jnp.logical_not(self.top)
        self.left = lax.rem(lon + N_LON - 1, N_LON)
        self.right = lax.rem(lon + 1, N_LON)
        self.up = jnp.where(self.top, lat, lat + 1)
        self.down = jnp.where(self.low, lat - 1, lat)
        self.f0 = jnp.where(self.top, N_LON - 1 - lon, lon)
        self.fl = jnp.where(self.top, lax.rem(N_LON - lon, N_LON), self.left)
        self.fr = jnp.where(self.top, lax.rem(2 * N_LON - 2 - lon, N_LON), self.right)
        self.far_l = jnp.logical_not(self.top & (self.fl == lon))
        self.far_r = jnp.logical_not(self.top & (self.fr == lon))

    def greet(self):
        barrier = pltpu.get_barrier_semaphore()

        def signal(a, b):
            pl.semaphore_signal(barrier, inc=1, device_id=(a, b), device_id_type=MESH)

        def along_lon(d, _):
            signal(self.lat, lax.rem(self.lon + d, N_LON))
            return 0

        def along_lat(d, _):
            signal(lax.rem(self.lat + d, N_LAT), self.lon)
            return 0

        lax.fori_loop(1, N_LON, along_lon, 0)
        lax.fori_loop(1, N_LAT, along_lat, 0)

        @pl.when(self.inner)
        def _():
            signal(self.up, self.left)
            signal(self.up, self.right)

        @pl.when(self.low)
        def _():
            signal(self.down, self.left)
            signal(self.down, self.right)

    def met(self):
        count = N_LON + N_LAT - 2 + jnp.where(self.inner, 2, 0) + jnp.where(self.low, 2, 0)
        pl.semaphore_wait(pltpu.get_barrier_semaphore(), count)


def copy(src, dst, send, recv, a, b):
    return pltpu.make_async_remote_copy(src_ref=src, dst_ref=dst, send_sem=send, recv_sem=recv,
                                        device_id=(a, b), device_id_type=MESH)


def when(cond, todo):
    @pl.when(cond)
    def _():
        todo()


class ColumnExchange:
    def __init__(self, lk, lcols, rcols, hc, rows, send, recv, base):
        to_l, to_r = pl.ds(0, 16), pl.ds(16, 16)
        self.copies = []
        for k, (start, n) in enumerate(rows):
            own, dst = pl.ds(start, n), pl.ds(start + 3, n)
            s = base + 2 * k
            self.copies += [copy(rcols.at[own], hc.at[dst, to_l], send.at[s], recv.at[s], lk.lat, lk.right),
                            copy(lcols.at[own], hc.at[dst, to_r], send.at[s + 1], recv.at[s + 1], lk.lat, lk.left)]

    def start(self):
        for c in self.copies:
            c.start()

    def wait(self):
        for c in self.copies:
            c.wait()


class RowExchange:
    def __init__(self, lk, first, last, to_lo, to_hi, to_fold, lcols, rcols, hc, send, recv):
        self.lk = lk
        lo, hi = pl.ds(0, 3), pl.ds(ROWS + 3, 3)
        to_l, to_r = pl.ds(0, 16), pl.ds(16, 16)
        l_first, l_last = lcols.at[pl.ds(0, 3)], lcols.at[pl.ds(ROWS - 3, 3)]
        r_first, r_last = rcols.at[pl.ds(0, 3)], rcols.at[pl.ds(ROWS - 3, 3)]
        self.up_n = copy(last, to_lo, send.at[1], recv.at[0], lk.up, lk.f0)
        self.up_f = copy(last, to_fold, send.at[1], recv.at[1], lk.up, lk.f0)
        self.ul_n = copy(l_last, hc.at[lo, to_r], send.at[4], recv.at[3], lk.up, lk.fl)
        self.ul_f = copy(l_last, hc.at[hi, to_l], send.at[4], recv.at[4], lk.up, lk.fl)
        self.ur_n = copy(r_last, hc.at[lo, to_l], send.at[5], recv.at[2], lk.up, lk.fr)
        self.ur_f = copy(r_last, hc.at[hi, to_r], send.at[5], recv.at[5], lk.up, lk.fr)
        self.dn = copy(first, to_hi, send.at[0], recv.at[1], lk.down, lk.lon)
        self.dl = copy(l_first, hc.at[hi, to_r], send.at[2], recv.at[5], lk.down, lk.left)
        self.dr = copy(r_first, hc.at[hi, to_l], send.at[3], recv.at[4], lk.down, lk.right)
        self.own_l = pltpu.make_async_copy(l_last, hc.at[hi, to_l], send.at[4])
        self.own_r = pltpu.make_async_copy(r_last, hc.at[hi, to_r], send.at[5])

    def start(self):
        lk = self.lk

        def inner():
            self.ul_n.start()
            self.ur_n.start()
            self.up_n.start()

        def low():
            self.dl.start()
            self.dr.start()
            self.dn.start()

        when(lk.inner, inner)
        when(lk.top & lk.far_l, self.ul_f.start)
        when(lk.top & lk.far_r, self.ur_f.start)
        when(jnp.logical_not(lk.far_l), self.own_l.start)
        when(jnp.logical_not(lk.far_r), self.own_r.start)
        when(lk.top, self.up_f.start)
        when(lk.low, low)

    def wait(self):
        lk = self.lk

        def low():
            self.up_n.wait_recv()
            self.ul_n.wait_recv()
            self.ur_n.wait_recv()
            self.dn.wait_send()
            self.dl.wait_send()
            self.dr.wait_send()

        when(lk.inner, self.dn.wait_recv)
        when(lk.top, self.up_f.wait_recv)
        when(lk.far_l, self.dr.wait_recv)
        when(lk.far_r, self.dl.wait_recv)
        when(jnp.logical_not(lk.far_l), self.own_l.wait)
        when(jnp.logical_not(lk.far_r), self.own_r.wait)
        when(lk.low, low)
        self.up_n.wait_send()
        when(lk.far_l, self.ul_n.wait_send)
        when(lk.far_r, self.ur_n.wait_send)


def fan(make, n, wait):
    def go(d, _):
        if wait:
            make(d).wait()
        else:
            make(d).start()
        return 0

    lax.fori_loop(1, n, go, 0)


def kernel(x, mask, cot_hbm, taps1, bias, gain, w_in, w_out, scale,
           upd_hbm, out_hbm, o_in, o_out, o_k, o_bias, o_gain,
           cot, upd, out, ext, ext2, wmat, taps, perm, rim_a, rim_b, w_in_t, w_out_t,
           raw_s, edge, hr, hc, hr2, hc2, fold, gin, gout, gks, small,
           wb, c1, c2, c3, r1, r2, r3, q1, q2,
           io, cs, cr, rs, rr, cs2, cr2, rs2, rr2, a1, b1, a2, b2, a3, b3, a4, b4, a5, b5):
    lk = Links()
    lat, lon = lk.lat, lk.lon
    for cond, e0 in ((jnp.logical_not(lk.low), 0), (lk.top, ROWS + 3)):
        @pl.when(cond)
        def _():
            for e in range(3):
                ext2[e0 + e] = jnp.zeros((22, 16, C), bf16)

    lk.greet()
    cot_in = pltpu.make_async_copy(cot_hbm, cot, io.at[0])
    cot_in.start()

    lane = iota2((1, COLS), 1)
    h32 = iota2((1, 32), 1)
    perm[...] = one_hot(swap(iota2((COLS, 1), 0)) == lane)
    place = rim_place()
    rim_a[...] = one_hot(place == lane)
    rim_b[...] = one_hot(place == jnp.where(h32 < 16, h32 - 16, 240 + h32))

    cols1 = ColumnExchange(lk, x.at[:, pl.ds(0, 16)], x.at[:, pl.ds(COLS - 16, 16)], hc, [(0, ROWS)], cs, cr, 0)
    rows1 = RowExchange(lk, x.at[pl.ds(0, 3)], x.at[pl.ds(ROWS - 3, 3)], hr.at[pl.ds(0, 3)], hr.at[pl.ds(3, 3)],
                        hr.at[pl.ds(3, 3)], x.at[:, pl.ds(0, 16)], x.at[:, pl.ds(COLS - 16, 16)], hc, rs, rr)
    lk.met()
    cols1.start()
    rows1.start()

    for t in range(49):
        taps[t] = jnp.broadcast_to(taps1[t // 7, t % 7:t % 7 + 1], (16, C))
    eye = one_hot(iota2((C, 1), 0) == iota2((1, C), 1))
    zero = jnp.zeros((C, C), bf16)
    for j in range(4):
        for b in range(7):
            for i in range(2):
                for o in range(2):
                    a = 2 * j + i - o
                    blk = eye * taps1[a, b:b + 1] if 0 <= a < 7 else zero
                    r0 = (j * 7 + b) * 256 + i * C
                    wmat[r0:r0 + C, o * C:(o + 1) * C] = blk
    w_in_t[...] = w_in[...].T
    w_out_t[...] = w_out[...].T
    for ref in (gin, gout, small, gks):
        ref[...] = jnp.zeros_like(ref)

    def build(j, _):
        full = dot(perm[...], jnp.concatenate([x[2 * j], x[2 * j + 1]], axis=-1)).astype(bf16)
        ext[2 * j + 3, 3:19] = full[:, :C].reshape(16, 16, C)
        ext[2 * j + 4, 3:19] = full[:, C:].reshape(16, 16, C)
        return 0

    lax.fori_loop(0, NB, build, 0)

    def put_rim(dst, e, rim):
        rim = rim.astype(bf16).reshape(6, 16, C)
        dst[e, 0:3] = rim[0:3]
        dst[e, 19:22] = rim[3:6]

    def rims1(j, _):
        main = jnp.concatenate([x[2 * j], x[2 * j + 1]], axis=-1)
        side = jnp.concatenate([hc[2 * j + 3], hc[2 * j + 4]], axis=-1)
        rim = dot(rim_a[...], main) + dot(rim_b[...], side)
        put_rim(ext, 2 * j + 3, rim[:, :C])
        put_rim(ext, 2 * j + 4, rim[:, C:])
        return 0

    cols1.wait()
    lax.fori_loop(0, NB, rims1, 0)
    cot_in.wait()

    def edges1():
        rows1.wait()
        zero_m = jnp.zeros((COLS, C), bf16)
        zero_s = jnp.zeros((32, C), bf16)
        for e in range(3):
            main = jnp.where(lk.low, hr[e], zero_m)
            side = jnp.where(lk.low, hc[e], zero_s)
            ext[e, 3:19] = dot(perm[...], main).astype(bf16).reshape(16, 16, C)
            put_rim(ext, e, dot(rim_a[...], main) + dot(rim_b[...], side))
        where = jnp.where(lk.top, 255 - lane, lane)
        own = one_hot(swap(iota2((COLS, 1), 0)) == where)
        ra = one_hot(place == where)
        side_col = jnp.where(lk.top, jnp.where(h32 < 16, -1 - h32, 287 - h32), jnp.where(h32 < 16, h32 - 16, 240 + h32))
        rb = one_hot(place == side_col)
        for m in range(3):
            src = jnp.where(lk.top, 2 - m, m)
            main = hr[3 + src]
            ext[35 + m, 3:19] = dot(own, main).astype(bf16).reshape(16, 16, C)
            put_rim(ext, 35 + m, dot(ra, main) + dot(rb, hc[35 + src]))

    cut = [(0, 18), (28, 4)]
    l_edge, r_edge = edge.at[:, pl.ds(0, 16)], edge.at[:, pl.ds(16, 16)]
    cols2a = ColumnExchange(lk, l_edge, r_edge, hc2, cut, cs2, cr2, 0)
    cols2b = ColumnExchange(lk, l_edge, r_edge, hc2, [(18, 10)], cs2, cr2, 4)
    rows2 = RowExchange(lk, ext2.at[pl.ds(3, 3), pl.ds(3, 16)], ext2.at[pl.ds(ROWS, 3), pl.ds(3, 16)],
                        ext2.at[pl.ds(0, 3), pl.ds(3, 16)], ext2.at[pl.ds(ROWS + 3, 3), pl.ds(3, 16)], hr2,
                        l_edge, r_edge, hc2, rs2, rr2)

    def sends2():
        cols2a.start()
        rows2.start()

    ones = jnp.ones((COLS, C), bf16)

    hs = iota2((32, 1), 0)
    sel = one_hot(jnp.where(hs < 16, hs, 224 + hs) == swap(lane))

    def block_work(new, old, slot):
        state = [None, 0]

        def conv(n):
            lo = state[1]
            part = conv_part(ext, new * R, wmat, False, lo, lo + n)
            state[0] = part if lo == 0 else state[0] + part
            state[1] = lo + n

        units, invs, norms, ups, masks = [], [], [], [], []
        for r in range(R):
            row = old * R + r
            raw = raw_s[1 - slot, :, r * C:(r + 1) * C] + bias[...]
            centre = jnp.mean(raw, axis=-1, keepdims=True)
            shifted = raw - centre
            var = jnp.mean(shifted * shifted, axis=-1, keepdims=True)
            inv = lax.rsqrt(var + epsilon)
            unit = shifted * inv
            units.append(unit)
            invs.append(inv)
            norms.append((unit * gain[...]).astype(bf16))
            pmask = perm[...] * mask[pl.ds(row, 1), :].astype(f32).astype(bf16)
            pair = dot(pmask, jnp.concatenate([cot[row], ones], axis=-1))
            ups.append(pair[:, :C].astype(bf16))
            masks.append(pair[:, C:])
            conv(CHUNKS[r])
        jobs = [(r, f) for r in range(R) for f in range(0, HID, 256)]

        def first(job):
            r, f = job
            return dot(norms[r], w_in[:, f:f + 256]), dot(ups[r], w_out_t[:, f:f + 256])

        mixed, bn = [None] * R, [None] * R
        ready = first(jobs[0])
        for q, (r, f) in enumerate(jobs):
            pre, bh = ready
            conv(CHUNKS[R + q])
            if q + 1 < len(jobs):
                ready = first(jobs[q + 1])
            act, der = gelu_parts(pre)
            hid = act.astype(bf16)
            bp = (bh * der).astype(bf16)
            mx = dot(hid, w_out[f:f + 256])
            bx = dot(bp, w_in_t[f:f + 256])
            mixed[r] = mx if mixed[r] is None else mixed[r] + mx
            bn[r] = bx if bn[r] is None else bn[r] + bx
            gin[:, f:f + 256] += dot_t(norms[r], bp)
            gout[:, f:f + 256] += dot_t(ups[r], hid)
        conv(28 - state[1])
        raw_s[slot] = state[0]
        bcs = []
        for r in range(R):
            unit = units[r]
            bnf = bn[r].astype(bf16).astype(f32)
            g = bnf * gain[...]
            m1 = jnp.mean(g, axis=-1, keepdims=True)
            m2 = jnp.mean(g * unit, axis=-1, keepdims=True)
            bc = ((g - m1 - unit * m2) * invs[r]).astype(bf16)
            small[0:8] += jnp.sum((bnf * unit).reshape(COLS // 8, 8, C), axis=0)
            small[8:16] += jnp.sum(bc.astype(f32).reshape(COLS // 8, 8, C), axis=0)
            ext2[old * R + r + 3, 3:19] = bc.reshape(16, 16, C)
            bcs.append(bc)
        nat = dot(perm[...], jnp.concatenate([(mixed[r] * masks[r]).astype(bf16) for r in range(R)], axis=-1))
        ends = dot(sel, jnp.concatenate(bcs, axis=-1)).astype(bf16)
        for r in range(R):
            row = old * R + r
            upd[row] = (x[row].astype(f32) + nat[:, r * C:(r + 1) * C]).astype(bf16)
            edge[row] = ends[:, r * C:(r + 1) * C]

    def main_step(n, _):
        when(n == FIRST, edges1)
        when(n == FIRST + 5, sends2)
        block_work(main_block(jnp.minimum(n, NB - 1)), main_block(jnp.maximum(n - 1, 0)), n % 2)
        return 0

    raw_s[0] = conv_part(ext, main_block(0) * R, wmat, False, 0, 28)
    lax.fori_loop(1, NB + 1, main_step, 0)

    upd_out = pltpu.make_async_copy(upd, upd_hbm, io.at[1])
    upd_out.start()
    cols2b.start()

    def hop1(d):
        to = lax.rem(lon + d, N_LON)
        return copy(wb.at[to], r1.at[d], a1.at[d], b1.at[d], lat, to)

    def hop2(d):
        return copy(c1, r2.at[lat], a2.at[d], b2.at[d], lax.rem(lat + d, N_LAT), lon)

    def hop3(d):
        return copy(c2, r3.at[lon], a3.at[d], b3.at[d], lat, lax.rem(lon + d, N_LON))

    def hop4(d):
        return copy(c3, q1.at[lon], a4.at[d], b4.at[d], lat, lax.rem(lon + d, N_LON))

    def hop5(d):
        return copy(c3, q2.at[lat], a5.at[d], b5.at[d], lax.rem(lat + d, N_LAT), lon)

    for c in range(N_LON):
        r0, c0 = c // 4 * 32, c % 4 * C
        wb[c, 0:32] = gin[r0:r0 + 32, c0:c0 + C].astype(bf16)
        wb[c, 32:SEG] = gout[r0:r0 + 32, c0:c0 + C].astype(bf16)
    fan(hop1, N_LON, False)

    def w_second():
        fan(hop1, N_LON, True)
        total = wb[lon].astype(f32)
        for d in range(1, N_LON):
            total = total + r1[d].astype(f32)
        c1[...] = total.astype(bf16)
        r2[lat] = c1[...]
        fan(hop2, N_LAT, False)

    def w_third():
        fan(hop2, N_LAT, True)
        total = r2[0].astype(f32)
        for d in range(1, N_LAT):
            total = total + r2[d].astype(f32)
        c2[...] = (total * scale[0]).astype(bf16)
        r3[lon] = c2[...]
        fan(hop3, N_LON, False)

    def rim2(e, row):
        main = ext2[e, 3:19].reshape(COLS, C)
        ra = one_hot(place == swap(lane))
        put_rim(ext2, e, dot(ra, main) + dot(rim_b[...], hc2[e]))

    def rims2(j, _):
        ra = one_hot(place == swap(lane))
        main = jnp.concatenate([ext2[2 * j + 3, 3:19].reshape(COLS, C), ext2[2 * j + 4, 3:19].reshape(COLS, C)], axis=-1)
        side = jnp.concatenate([hc2[2 * j + 3], hc2[2 * j + 4]], axis=-1)
        rim = dot(ra, main) + dot(rim_b[...], side)
        put_rim(ext2, 2 * j + 3, rim[:, :C])
        put_rim(ext2, 2 * j + 4, rim[:, C:])
        return 0

    cols2a.wait()
    lax.fori_loop(0, 9, rims2, 0)
    lax.fori_loop(14, 16, rims2, 0)

    def late_cols():
        cols2b.wait()
        lax.fori_loop(9, 14, rims2, 0)

    def edges2():
        rows2.wait()
        ra = one_hot(place == swap(lane))

        def rim(e):
            put_rim(ext2, e, dot(ra, ext2[e, 3:19].reshape(COLS, C)) + dot(rim_b[...], hc2[e]))

        def low():
            for e in range(3):
                rim(e)

        def inner():
            for e in range(3):
                rim(35 + e)

        def top():
            own = one_hot(swap(iota2((COLS, 1), 0)) == 255 - swap(lane))
            fa = one_hot(place == 255 - swap(lane))
            fb = one_hot(place == jnp.where(h32 < 16, -1 - h32, 287 - h32))
            for m in range(3):
                main = hr2[2 - m].reshape(COLS, C)
                fold[m, 3:19] = dot(own, main).astype(bf16).reshape(16, 16, C)
                put_rim(fold, m, dot(fa, main) + dot(fb, hc2[37 - m]))

        when(lk.low, low)
        when(lk.inner, inner)
        when(lk.top, top)

    def tap_sums(src, e, row, a, flip):
        for b in range(7):
            total = None
            for k0 in (0, 8):
                q = src[e, k0 + b] * ext[row + 3, 3 + k0]
                for k in range(k0 + 1, k0 + 8):
                    q = q + src[e, k + b] * ext[row + 3, 3 + k]
                total = q if total is None else total + q
            q = total.astype(f32)
            t = a * 7 + b
            gks[(48 - t) if flip else t] += q[:8] + q[8:]

    def back_step(n, _):
        when(n == 5, late_cols)
        when(n == 6, w_second)
        when(n == 11, w_third)
        when(n == 12, edges2)
        row = back_block(n) * R
        conv = None
        for j in range(4):
            part = conv_part(ext2, row, wmat, True, 7 * j, 7 * j + 7)
            conv = part if conv is None else conv + part
            if j == 3:
                nat = dot(perm[...], conv.astype(bf16))
            for t in range((7 * j + 1) // 2, (7 * j + 8) // 2):
                tap_sums(ext2, row + t // 7 + t % 7, row + t // 7, t % 7, True)
        for r in range(R):
            out[row + r] = (cot[row + r].astype(f32) + nat[:, (1 - r) * C:(2 - r) * C]).astype(bf16)
        return 0

    lax.fori_loop(0, NB, back_step, 0)

    @pl.when(lk.top)
    def _():
        for t in range(3):
            row = ROWS - 3 + t
            acc = [None] * 16
            for m in range(t + 1):
                a = 6 - t + m
                for k in range(16):
                    p = fold[m, k] * taps[a * 7]
                    for b in range(1, 7):
                        p = p + fold[m, k + b] * taps[a * 7 + b]
                    p = p.astype(f32)
                    acc[k] = p if acc[k] is None else acc[k] + p
                tap_sums(fold, m, row, a, False)
            more = dot(perm[...], jnp.concatenate(acc, axis=0).astype(bf16))
            out[row] = (out[row].astype(f32) + more).astype(bf16)

    out_out = pltpu.make_async_copy(out, out_hbm, io.at[0])
    out_out.start()

    c3[...] = jnp.zeros_like(c3)
    rest = [jnp.sum(gks[t], axis=0, keepdims=True) for t in range(49)]
    rest += [jnp.sum(small[:8], axis=0, keepdims=True), jnp.sum(small[8:], axis=0, keepdims=True), jnp.zeros((13, C), f32)]
    c3[...] = jnp.concatenate(rest, axis=0).astype(bf16)
    fan(hop4, N_LON, False)
    q1[lon] = c3[...]
    fan(hop3, N_LON, True)
    for j in range(4):
        for k in range(4):
            o_in[32 * k:32 * k + 32, j * C:(j + 1) * C] = r3[4 * k + j, 0:32].astype(f32)
        whole = jnp.concatenate([r3[4 * k + j, 32:SEG] for k in range(4)], axis=0).astype(f32)
        o_out[j * C:(j + 1) * C] = whole.T
    fan(hop4, N_LON, True)
    total = q1[0].astype(f32)
    for d in range(1, N_LON):
        total = total + q1[d].astype(f32)
    c3[...] = total.astype(bf16)
    fan(hop5, N_LAT, False)
    q2[lat] = c3[...]
    fan(hop5, N_LAT, True)
    total = q2[0].astype(f32)
    for d in range(1, N_LAT):
        total = total + q2[d].astype(f32)
    total = total * scale[0]
    for a in range(7):
        o_k[a] = total[7 * a:7 * a + 7]
    o_gain[...] = total[49:50]
    o_bias[...] = total[50:51]
    upd_out.wait()
    out_out.wait()


def body(ocean_state, sea_mask, depth_kernel, conv_bias, norm_gain, w_in, w_out, cotangent):
    cells = COLS * ROWS * lax.axis_size("lat") * lax.axis_size("lon")
    scale = 1.0 / jnp.sqrt(jnp.full((1,), cells, f32))
    vm = pl.BlockSpec(memory_space=pltpu.VMEM)
    hbm = pl.BlockSpec(memory_space=pl.ANY)
    dma = pltpu.SemaphoreType.DMA
    V = pltpu.VMEM
    tile = jax.ShapeDtypeStruct((ROWS, COLS, C), bf16)
    upd, grad_state, o_in, o_out, o_k, o_bias, o_gain = pl.pallas_call(
        kernel,
        in_specs=[vm, vm, hbm, vm, vm, vm, vm, vm, pl.BlockSpec(memory_space=pltpu.SMEM)],
        out_specs=[hbm, hbm] + [vm] * 5,
        out_shape=[tile, tile, jax.ShapeDtypeStruct((C, HID), f32), jax.ShapeDtypeStruct((HID, C), f32),
                   jax.ShapeDtypeStruct((7, 7, C), f32), jax.ShapeDtypeStruct((1, C), f32), jax.ShapeDtypeStruct((1, C), f32)],
        scratch_shapes=[
            V((ROWS, COLS, C), bf16), V((ROWS, COLS, C), bf16), V((ROWS, COLS, C), bf16),
            V((38, 22, 16, C), bf16), V((38, 22, 16, C), bf16), V((28 * 256, 256), bf16), V((49, 16, C), bf16),
            V((COLS, COLS), bf16), V((96, COLS), bf16), V((96, 32), bf16), V((HID, C), bf16), V((C, HID), bf16),
            V((2, COLS, R * C), f32),
            V((ROWS, 32, C), bf16), V((6, COLS, C), bf16), V((ROWS + 6, 32, C), bf16),
            V((3, 16, 16, C), bf16), V((ROWS + 6, 32, C), bf16), V((3, 22, 16, C), bf16),
            V((C, HID), f32), V((C, HID), f32), V((49, 8, C), f32), V((16, C), f32),
            V((N_LON, SEG, C), bf16), V((SEG, C), bf16), V((SEG, C), bf16), V((SEG, C), bf16),
            V((N_LON, SEG, C), bf16), V((N_LAT, SEG, C), bf16), V((N_LON, SEG, C), bf16),
            V((N_LON, SEG, C), bf16), V((N_LAT, SEG, C), bf16),
            dma((2,)), dma((2,)), dma((2,)), dma((6,)), dma((6,)), dma((6,)), dma((6,)), dma((6,)), dma((6,)),
            dma((N_LON,)), dma((N_LON,)), dma((N_LAT,)), dma((N_LAT,)), dma((N_LON,)), dma((N_LON,)),
            dma((N_LON,)), dma((N_LON,)), dma((N_LAT,)), dma((N_LAT,))],
        compiler_params=pltpu.CompilerParams(collective_id=0, has_side_effects=True, vmem_limit_bytes=VLIM),
        name="block_step",
    )(ocean_state, sea_mask, cotangent, depth_kernel, conv_bias.reshape(1, C), norm_gain.reshape(1, C), w_in, w_out, scale)
    return upd, grad_state, o_k, o_bias.reshape(C), o_gain.reshape(C), o_in, o_out


def solution(mesh):
    tile = P("lat", "lon", None)
    return jax.shard_map(
        body,
        mesh=mesh,
        in_specs=(tile, P("lat", "lon"), P(), P(), P(), P(), P(), tile),
        out_specs=(tile, tile, P(), P(), P(), P(), P()),
        check_vma=False,
    )
```

time: 434 us -> 122 us (0.28)
  other arithmetic: 147 us -> 0 us
  Pallas kernels: 0 us -> 113 us
  waiting for transfers between devices: 102 us -> 0 us
  blocking collectives: 67.8 us -> 0 us
  matrix products: 54.4 us -> 0 us
  starting transfers between devices: 33 us -> 0 us
  between operations: 15.6 us -> 0.68 us
    pallas_call x0 -> x1, Pallas kernels: none -> 113 us  [body(): pl.pallas_call(kernel, in_specs=[vm, vm, hbm, vm, vm, vm, vm, vm, pl.Bloc...]
    psum x1 -> x0, waiting for transfers between devices: 79.3 us -> none  [body(): lax.psum((kernel_grad, bias_grad, gain_part, in_part, out_part), ('lat',...]
    reduce_sum x5 -> x0, other arithmetic: 67.9 us -> none  [the longest x1 37.1 us: normalize(): centre = jnp.mean(conv_rows, axis=-1, keepdims=True)]
    psum x1 -> x0, blocking collectives: 67.8 us -> none  [body(): lax.psum((kernel_grad, bias_grad, gain_part, in_part, out_part), ('lat',...]
    dot_general x6 -> x0, matrix products: 54.4 us -> none  [the longest x1 19.4 us: column_mlp(): jnp.dot(hidden, w_out, preferred_element_type=jnp.float32)]
    add x3 -> x0, other arithmetic: 51.8 us -> none  [the longest x1 48.6 us: body(): state_grad = cotangent.astype(jnp.float32) + inner_grad]
    ppermute x16 -> x0, starting transfers between devices: 33 us -> none  [the longest x4 17 us: with_halo(): lax.ppermute(lax.slice_in_dim(block, block.shape[dim] - width, None, axis...]
    ppermute x16 -> x0, waiting for transfers between devices: 22.2 us -> none  [the longest x8 17.7 us: partner(): return lax.ppermute(value, axis, pairs)]
  transfers between devices with their start and end apart: 17 -> 0, of which waited for: 9 -> 0; matrix products, arithmetic and copies ran while one was open for 17% -> 0% of each run, Pallas kernels for 0% -> 0%
where the time goes in v3:
time: 122 us
  Pallas kernels  113 us (93%)
  local copies, waits for them, and re-layouts  7.67 us (6%)
    pallas_call x1, Pallas kernels, body(): pl.pallas_call(kernel, in_specs=[vm, vm, hbm, vm, vm, vm, vm, vm, pl.Bloc...  113 us
    unnamed x19, local copies, waits for them, and re-layouts  7.67 us

profile of v3, /device:TPU:1, one launch (start us, length us, event | category | flops | bytes accessed | tf_op | source)
XLA Modules:
  0.0 121.6 jit_solution(4452340760151184963)
XLA Ops:
  0.6 113.3 %block_step.1 = (bf16[32,256,128]{2,1,0:T(8,128)(2,1)}, bf16[32,256,128]{2,1,0:T(8,128)(2,1)}, f32[128,512]{1,0:T(8,128)}, f32[512,128]{1,0:T(8,128)}, f32[7,7,1...) custom-call(bf16[32,256,128]{2,1,0:T(8,128)(2,1)} %x.1, s32[32,256]{1,0:T(8,128)} %mask.1, ...), custom_call_target="tpu_custom_call" | custom-call | tf_op jit(solution)/shard_map/block_step/pallas_call | solution.py:618
  113.9 0.0 copy-start
  113.9 3.3 %copy.22 = bf16[32,256,128]{2,1,0:T(8,128)(2,1)} copy(bf16[32,256,128]{2,1,0:T(8,128)(2,1)} %get-tuple-element.28) | data formatting | bytes 4194304
  117.2 0.0 copy-done
  117.2 0.0 copy-start.3
  117.2 0.0 copy-start.5
  117.2 0.0 copy-start.4
  117.2 0.0 copy-start.2
  117.2 0.0 copy-start.1
  117.3 1.3 %copy.23 = bf16[32,256,128]{2,1,0:T(8,128)(2,1)} copy(bf16[32,256,128]{2,1,0:T(8,128)(2,1)S(1)} %copy-done) | data formatting | bytes 4194304
  118.6 0.0 copy-done.3
  118.6 0.6 copy.24
  119.2 0.0 copy-done.5
  119.2 0.5 copy.25
  119.7 0.0 copy-done.4
  119.7 0.5 copy.26
  120.2 0.0 copy-done.2
  120.2 0.7 copy.27
  120.9 0.0 copy-done.1
  120.9 0.7 copy.28
Async XLA Ops:
  113.9 3.3 %copy-start = (bf16[32,256,128]{2,1,0:T(8,128)(2,1)S(1)}, bf16[32,256,128]{2,1,0:T(8,128)(2,1)}, u32[]{:S(2)}) copy-start(bf16[32,256,128]{2,1,0:T(8,128)(2,1)} %get-tuple-element.29) | copy-start | bytes 6291460
  117.2 1.4 %copy-start.3 = (f32[7,7,128]{2,1,0:T(8,128)S(1)}, f32[7,7,128]{2,1,0:T(8,128)}, u32[]{:S(2)}) copy-start(f32[7,7,128]{2,1,0:T(8,128)} %get-tuple-element.30) | copy-start | bytes 75268
  117.2 2.0 %copy-start.5 = (f32[1,128]{1,0:T(1,128)S(1)}, f32[1,128]{1,0:T(1,128)}, u32[]{:S(2)}) copy-start(f32[1,128]{1,0:T(1,128)} %get-tuple-element.17) | copy-start | bytes 1540
  117.2 2.5 %copy-start.4 = (f32[1,128]{1,0:T(1,128)S(1)}, f32[1,128]{1,0:T(1,128)}, u32[]{:S(2)}) copy-start(f32[1,128]{1,0:T(1,128)} %get-tuple-element.18) | copy-start | bytes 1540
  117.2 3.0 %copy-start.2 = (f32[128,512]{1,0:T(8,128)S(1)}, f32[128,512]{1,0:T(8,128)}, u32[]{:S(2)}) copy-start(f32[128,512]{1,0:T(8,128)} %get-tuple-element.33) | copy-start | bytes 786436
  117.2 3.7 %copy-start.1 = (f32[512,128]{1,0:T(8,128)S(1)}, f32[512,128]{1,0:T(8,128)}, u32[]{:S(2)}) copy-start(f32[512,128]{1,0:T(8,128)} %get-tuple-element.34) | copy-start | bytes 786436

commit v4 on v3

--- a/solution.py
+++ b/solution.py
@@ -12,6 +12,8 @@
 epsilon = 1e-06
 root_half = 0.7978845608028654
 cubic_coef = 0.044715
+z_one = -2.0 * root_half * 1.4426950408889634
+z_three = -2.0 * root_half * cubic_coef * 1.4426950408889634
 
 C = 128
 ROWS = 32
@@ -21,11 +23,10 @@
 N_LON = 16
 N_LAT = 8
 SEG = 64
-R = 2
-M = R * COLS
+R = 4
 NB = ROWS // R
-FIRST = 7
-CHUNKS = (3, 3, 4, 4, 5, 5)
+FIRST = 3
+MX_TAPS = 14
 VLIM = 60 * 1024 * 1024
 
 
@@ -56,34 +57,63 @@
 
 
 def conv_part(ext, row, wmat, flip, lo, hi):
-    parts = []
-    for u in range(lo, hi):
-        j, b = u // 7, u % 7
-        e = row + 2 * (3 - j if flip else j)
-        s = 6 - b if flip else b
-        pair = [ext[e, s:s + 16].reshape(COLS, C), ext[e + 1, s:s + 16].reshape(COLS, C)]
-        parts += pair[::-1] if flip else pair
-    return dot(jnp.concatenate(parts, axis=-1), wmat[lo * 256:hi * 256])
+    sides = []
+    for pair_row in (row, row + 2):
+        parts = []
+        for u in range(lo, hi):
+            j, b = u // 7, u % 7
+            e = pair_row + 2 * (3 - j if flip else j)
+            s = 6 - b if flip else b
+            pair = [ext[e, s:s + 16].reshape(COLS, C), ext[e + 1, s:s + 16].reshape(COLS, C)]
+            parts += pair[::-1] if flip else pair
+        sides.append(jnp.concatenate(parts, axis=-1))
+    return dot(jnp.concatenate(sides, axis=0), wmat[lo * 256:hi * 256])
+
+
+def conv_rest(ext, taps, row, o, k0, dst):
+    acc = [None] * 8
+    for a in range(MX_TAPS // 7 * 2 - o, 7):
+        win = [ext[row + a, k0 + k] for k in range(14)]
+        w = [taps[a * 7 + b] for b in range(7)]
+        for k in range(8):
+            p = win[k] * w[0]
+            for b in range(1, 7):
+                p = p + win[k + b] * w[b]
+            p = p.astype(f32)
+            acc[k] = p if acc[k] is None else acc[k] + p
+    for k in range(8):
+        dst[(k0 + k) * 16:(k0 + k + 1) * 16] = acc[k]
+
+
+def conv_first(ext, taps, row, o):
+    acc = [None] * 16
+    for a in range(2 - o):
+        w = [taps[48 - a * 7 - b] for b in range(7)]
+        for k in range(16):
+            p = ext[row + o + a, k] * w[0]
+            for b in range(1, 7):
+                p = p + ext[row + o + a, k + b] * w[b]
+            p = p.astype(f32)
+            acc[k] = p if acc[k] is None else acc[k] + p
+    return jnp.concatenate(acc, axis=0)
 
 
 def gelu_parts(v):
     u = v * v
-    t = jnp.tanh(v * (root_half + (root_half * cubic_coef) * u))
-    h = 0.5 * t + 0.5
+    z = jnp.minimum(v * (z_one + z_three * u), 80.0)
+    e = jnp.exp2(z)
+    h = pl.reciprocal(e + 1.0, approx=True)
     act = v * h
-    der = h + act * (1.0 - h) * (2.0 * root_half + (6.0 * root_half * cubic_coef) * u)
+    der = h + (act * (e * h)) * (2.0 * root_half + (6.0 * root_half * cubic_coef) * u)
     return act, der
 
 
 def main_block(n):
-    late = n - FIRST
-    edge = jnp.where(late < 2, late, late + 12)
-    return jnp.where(n < FIRST, n + 2, jnp.where(late < 4, edge, n - 2))
+    return jnp.where(n < FIRST, n + 1, jnp.where(n == FIRST, 0, jnp.where(n == FIRST + 1, NB - 1, n - 1)))
 
 
 def back_block(n):
-    late = n - 12
-    return jnp.where(n < 12, n + 2, jnp.where(late < 2, late, late + 12))
+    return jnp.where(n < NB - 2, n + 1, jnp.where(n == NB - 2, 0, NB - 1))
 
 
 class Links:
@@ -243,7 +273,7 @@
 def kernel(x, mask, cot_hbm, taps1, bias, gain, w_in, w_out, scale,
            upd_hbm, out_hbm, o_in, o_out, o_k, o_bias, o_gain,
            cot, upd, out, ext, ext2, wmat, taps, perm, rim_a, rim_b, w_in_t, w_out_t,
-           raw_s, edge, hr, hc, hr2, hc2, fold, gin, gout, gks, small,
+           raw_s, rest_s, up_s, mask_s, last_s, edge, hr, hc, hr2, hc2, fold, gin, gout, gks, small,
            wb, c1, c2, c3, r1, r2, r3, q1, q2,
            io, cs, cr, rs, rr, cs2, cr2, rs2, rr2, a1, b1, a2, b2, a3, b3, a4, b4, a5, b5):
     lk = Links()
@@ -264,13 +294,6 @@
     place = rim_place()
     rim_a[...] = one_hot(place == lane)
     rim_b[...] = one_hot(place == jnp.where(h32 < 16, h32 - 16, 240 + h32))
-
-    cols1 = ColumnExchange(lk, x.at[:, pl.ds(0, 16)], x.at[:, pl.ds(COLS - 16, 16)], hc, [(0, ROWS)], cs, cr, 0)
-    rows1 = RowExchange(lk, x.at[pl.ds(0, 3)], x.at[pl.ds(ROWS - 3, 3)], hr.at[pl.ds(0, 3)], hr.at[pl.ds(3, 3)],
-                        hr.at[pl.ds(3, 3)], x.at[:, pl.ds(0, 16)], x.at[:, pl.ds(COLS - 16, 16)], hc, rs, rr)
-    lk.met()
-    cols1.start()
-    rows1.start()
 
     for t in range(49):
         taps[t] = jnp.broadcast_to(taps1[t // 7, t % 7:t % 7 + 1], (16, C))
@@ -289,30 +312,51 @@
     for ref in (gin, gout, small, gks):
         ref[...] = jnp.zeros_like(ref)
 
-    def build(j, _):
-        full = dot(perm[...], jnp.concatenate([x[2 * j], x[2 * j + 1]], axis=-1)).astype(bf16)
-        ext[2 * j + 3, 3:19] = full[:, :C].reshape(16, 16, C)
-        ext[2 * j + 4, 3:19] = full[:, C:].reshape(16, 16, C)
+    def build(t, _):
+        for j in (2 * t, 2 * t + 1):
+            full = dot(perm[...], jnp.concatenate([x[2 * j], x[2 * j + 1]], axis=-1)).astype(bf16)
+            ext[2 * j + 3, 3:19] = full[:, :C].reshape(16, 16, C)
+            ext[2 * j + 4, 3:19] = full[:, C:].reshape(16, 16, C)
         return 0
 
-    lax.fori_loop(0, NB, build, 0)
+    lax.fori_loop(0, ROWS // 4, build, 0)
+
+    cols1 = ColumnExchange(lk, x.at[:, pl.ds(0, 16)], x.at[:, pl.ds(COLS - 16, 16)], hc, [(0, ROWS)], cs, cr, 0)
+    rows1 = RowExchange(lk, x.at[pl.ds(0, 3)], x.at[pl.ds(ROWS - 3, 3)], hr.at[pl.ds(0, 3)], hr.at[pl.ds(3, 3)],
+                        hr.at[pl.ds(3, 3)], x.at[:, pl.ds(0, 16)], x.at[:, pl.ds(COLS - 16, 16)], hc, rs, rr)
+    lk.met()
+    cols1.start()
+    rows1.start()
+
+    ones = jnp.ones((COLS, C), bf16)
+
+    def mask_rows(t, _):
+        for row in (2 * t, 2 * t + 1):
+            pmask = perm[...] * mask[pl.ds(row, 1), :].astype(f32).astype(bf16)
+            pair = dot(pmask, jnp.concatenate([cot[row], ones], axis=-1)).astype(bf16)
+            up_s[row] = pair[:, :C]
+            mask_s[row] = pair[:, C:]
+        return 0
+
+    cot_in.wait()
+    lax.fori_loop(0, ROWS // 2, mask_rows, 0)
 
     def put_rim(dst, e, rim):
         rim = rim.astype(bf16).reshape(6, 16, C)
         dst[e, 0:3] = rim[0:3]
         dst[e, 19:22] = rim[3:6]
 
-    def rims1(j, _):
-        main = jnp.concatenate([x[2 * j], x[2 * j + 1]], axis=-1)
-        side = jnp.concatenate([hc[2 * j + 3], hc[2 * j + 4]], axis=-1)
-        rim = dot(rim_a[...], main) + dot(rim_b[...], side)
-        put_rim(ext, 2 * j + 3, rim[:, :C])
-        put_rim(ext, 2 * j + 4, rim[:, C:])
+    def rims1(t, _):
+        for j in (2 * t, 2 * t + 1):
+            main = jnp.concatenate([x[2 * j], x[2 * j + 1]], axis=-1)
+            side = jnp.concatenate([hc[2 * j + 3], hc[2 * j + 4]], axis=-1)
+            rim = dot(rim_a[...], main) + dot(rim_b[...], side)
+            put_rim(ext, 2 * j + 3, rim[:, :C])
+            put_rim(ext, 2 * j + 4, rim[:, C:])
         return 0
 
     cols1.wait()
-    lax.fori_loop(0, NB, rims1, 0)
-    cot_in.wait()
+    lax.fori_loop(0, ROWS // 4, rims1, 0)
 
     def edges1():
         rows1.wait()
@@ -334,10 +378,10 @@
             ext[35 + m, 3:19] = dot(own, main).astype(bf16).reshape(16, 16, C)
             put_rim(ext, 35 + m, dot(ra, main) + dot(rb, hc[35 + src]))
 
-    cut = [(0, 18), (28, 4)]
+    cut = [(0, 16), (28, 4)]
     l_edge, r_edge = edge.at[:, pl.ds(0, 16)], edge.at[:, pl.ds(16, 16)]
     cols2a = ColumnExchange(lk, l_edge, r_edge, hc2, cut, cs2, cr2, 0)
-    cols2b = ColumnExchange(lk, l_edge, r_edge, hc2, [(18, 10)], cs2, cr2, 4)
+    cols2b = ColumnExchange(lk, l_edge, r_edge, hc2, [(16, 12)], cs2, cr2, 4)
     rows2 = RowExchange(lk, ext2.at[pl.ds(3, 3), pl.ds(3, 16)], ext2.at[pl.ds(ROWS, 3), pl.ds(3, 16)],
                         ext2.at[pl.ds(0, 3), pl.ds(3, 16)], ext2.at[pl.ds(ROWS + 3, 3), pl.ds(3, 16)], hr2,
                         l_edge, r_edge, hc2, rs2, rr2)
@@ -346,24 +390,22 @@
         cols2a.start()
         rows2.start()
 
-    ones = jnp.ones((COLS, C), bf16)
-
     hs = iota2((32, 1), 0)
     sel = one_hot(jnp.where(hs < 16, hs, 224 + hs) == swap(lane))
 
-    def block_work(new, old, slot):
-        state = [None, 0]
-
-        def conv(n):
-            lo = state[1]
-            part = conv_part(ext, new * R, wmat, False, lo, lo + n)
-            state[0] = part if lo == 0 else state[0] + part
-            state[1] = lo + n
-
-        units, invs, norms, ups, masks = [], [], [], [], []
+    def conv_block(blk):
+        part = conv_part(ext, blk * R, wmat, False, 0, 7)
         for r in range(R):
-            row = old * R + r
-            raw = raw_s[1 - slot, :, r * C:(r + 1) * C] + bias[...]
+            for k0 in (0, 8):
+                conv_rest(ext, taps, blk * R + r, r % 2, k0, rest_s.at[r])
+        part = part + conv_part(ext, blk * R, wmat, False, 7, 14)
+        raw_s[...] = part
+
+    def mlp_pair(blk, p):
+        units, invs, norms = [], [], []
+        top = p * COLS if isinstance(p, int) else pl.multiple_of(p * COLS, COLS)
+        for o in range(2):
+            raw = raw_s[pl.ds(top, COLS), o * C:(o + 1) * C] + rest_s[2 * p + o] + bias[...]
             centre = jnp.mean(raw, axis=-1, keepdims=True)
             shifted = raw - centre
             var = jnp.mean(shifted * shifted, axis=-1, keepdims=True)
@@ -372,62 +414,55 @@
             units.append(unit)
             invs.append(inv)
             norms.append((unit * gain[...]).astype(bf16))
-            pmask = perm[...] * mask[pl.ds(row, 1), :].astype(f32).astype(bf16)
-            pair = dot(pmask, jnp.concatenate([cot[row], ones], axis=-1))
-            ups.append(pair[:, :C].astype(bf16))
-            masks.append(pair[:, C:])
-            conv(CHUNKS[r])
-        jobs = [(r, f) for r in range(R) for f in range(0, HID, 256)]
-
-        def first(job):
-            r, f = job
-            return dot(norms[r], w_in[:, f:f + 256]), dot(ups[r], w_out_t[:, f:f + 256])
-
-        mixed, bn = [None] * R, [None] * R
-        ready = first(jobs[0])
-        for q, (r, f) in enumerate(jobs):
-            pre, bh = ready
-            conv(CHUNKS[R + q])
-            if q + 1 < len(jobs):
-                ready = first(jobs[q + 1])
-            act, der = gelu_parts(pre)
-            hid = act.astype(bf16)
-            bp = (bh * der).astype(bf16)
+        norm = jnp.concatenate(norms, axis=0)
+        first_row = blk * R + 2 * p
+        up = jnp.concatenate([up_s[first_row], up_s[first_row + 1]], axis=0)
+        mixed, bn = None, None
+        halves = range(0, HID, 256)
+        ready = [(dot(norm, w_in[:, f:f + 256]).astype(bf16), dot(up, w_out_t[:, f:f + 256]).astype(bf16)) for f in halves]
+        for f, (pre, bh) in zip(halves, ready):
+            hid, der = gelu_parts(pre)
+            bp = bh * der
             mx = dot(hid, w_out[f:f + 256])
             bx = dot(bp, w_in_t[f:f + 256])
-            mixed[r] = mx if mixed[r] is None else mixed[r] + mx
-            bn[r] = bx if bn[r] is None else bn[r] + bx
-            gin[:, f:f + 256] += dot_t(norms[r], bp)
-            gout[:, f:f + 256] += dot_t(ups[r], hid)
-        conv(28 - state[1])
-        raw_s[slot] = state[0]
+            mixed = mx if mixed is None else mixed + mx
+            bn = bx if bn is None else bn + bx
+            gin[:, f:f + 256] += dot_t(norm, bp)
+            gout[:, f:f + 256] += dot_t(up, hid)
+        mixed = mixed.astype(bf16)
         bcs = []
-        for r in range(R):
-            unit = units[r]
-            bnf = bn[r].astype(bf16).astype(f32)
+        for o in range(2):
+            half = slice(o * COLS, (o + 1) * COLS)
+            unit = units[o]
+            bnf = bn[half].astype(bf16).astype(f32)
             g = bnf * gain[...]
             m1 = jnp.mean(g, axis=-1, keepdims=True)
             m2 = jnp.mean(g * unit, axis=-1, keepdims=True)
-            bc = ((g - m1 - unit * m2) * invs[r]).astype(bf16)
+            bc = ((g - m1 - unit * m2) * invs[o]).astype(bf16)
             small[0:8] += jnp.sum((bnf * unit).reshape(COLS // 8, 8, C), axis=0)
             small[8:16] += jnp.sum(bc.astype(f32).reshape(COLS // 8, 8, C), axis=0)
-            ext2[old * R + r + 3, 3:19] = bc.reshape(16, 16, C)
+            ext2[first_row + o + 3, 3:19] = bc.reshape(16, 16, C)
             bcs.append(bc)
-        nat = dot(perm[...], jnp.concatenate([(mixed[r] * masks[r]).astype(bf16) for r in range(R)], axis=-1))
+        nat = dot(perm[...], jnp.concatenate([mixed[o * COLS:(o + 1) * COLS] * mask_s[first_row + o] for o in range(2)], axis=-1))
         ends = dot(sel, jnp.concatenate(bcs, axis=-1)).astype(bf16)
-        for r in range(R):
-            row = old * R + r
-            upd[row] = (x[row].astype(f32) + nat[:, r * C:(r + 1) * C]).astype(bf16)
-            edge[row] = ends[:, r * C:(r + 1) * C]
+        for o in range(2):
+            row = first_row + o
+            upd[row] = (x[row].astype(f32) + nat[:, o * C:(o + 1) * C]).astype(bf16)
+            edge[row] = ends[:, o * C:(o + 1) * C]
 
     def main_step(n, _):
         when(n == FIRST, edges1)
-        when(n == FIRST + 5, sends2)
-        block_work(main_block(jnp.minimum(n, NB - 1)), main_block(jnp.maximum(n - 1, 0)), n % 2)
+        when(n == FIRST + 2, sends2)
+        blk = main_block(n)
+        conv_block(blk)
+
+        @pl.when(n < NB)
+        def _():
+            for p in range(2):
+                mlp_pair(blk, p)
         return 0
 
-    raw_s[0] = conv_part(ext, main_block(0) * R, wmat, False, 0, 28)
-    lax.fori_loop(1, NB + 1, main_step, 0)
+    lax.fori_loop(0, NB, main_step, 0)
 
     upd_out = pltpu.make_async_copy(upd, upd_hbm, io.at[1])
     upd_out.start()
@@ -478,22 +513,23 @@
         ra = one_hot(place == swap(lane))
         put_rim(ext2, e, dot(ra, main) + dot(rim_b[...], hc2[e]))
 
-    def rims2(j, _):
+    def rims2(t, _):
         ra = one_hot(place == swap(lane))
-        main = jnp.concatenate([ext2[2 * j + 3, 3:19].reshape(COLS, C), ext2[2 * j + 4, 3:19].reshape(COLS, C)], axis=-1)
-        side = jnp.concatenate([hc2[2 * j + 3], hc2[2 * j + 4]], axis=-1)
-        rim = dot(ra, main) + dot(rim_b[...], side)
-        put_rim(ext2, 2 * j + 3, rim[:, :C])
-        put_rim(ext2, 2 * j + 4, rim[:, C:])
+        for j in (2 * t, 2 * t + 1):
+            main = jnp.concatenate([ext2[2 * j + 3, 3:19].reshape(COLS, C), ext2[2 * j + 4, 3:19].reshape(COLS, C)], axis=-1)
+            side = jnp.concatenate([hc2[2 * j + 3], hc2[2 * j + 4]], axis=-1)
+            rim = dot(ra, main) + dot(rim_b[...], side)
+            put_rim(ext2, 2 * j + 3, rim[:, :C])
+            put_rim(ext2, 2 * j + 4, rim[:, C:])
         return 0
 
     cols2a.wait()
-    lax.fori_loop(0, 9, rims2, 0)
-    lax.fori_loop(14, 16, rims2, 0)
+    lax.fori_loop(0, 4, rims2, 0)
+    rims2(7, 0)
 
     def late_cols():
         cols2b.wait()
-        lax.fori_loop(9, 14, rims2, 0)
+        lax.fori_loop(4, 7, rims2, 0)
 
     def edges2():
         rows2.wait()
@@ -535,30 +571,44 @@
             t = a * 7 + b
             gks[(48 - t) if flip else t] += q[:8] + q[8:]
 
+    def finish(t, _):
+        nat = dot(perm[...], last_s[t])
+        for o in range(2):
+            out[2 * t + o] = (cot[2 * t + o].astype(f32) + nat[:, (1 - o) * C:(2 - o) * C]).astype(bf16)
+        return 0
+
     def back_step(n, _):
-        when(n == 5, late_cols)
-        when(n == 6, w_second)
-        when(n == 11, w_third)
-        when(n == 12, edges2)
+        when(n == 2, late_cols)
+        when(n == 3, w_second)
+        when(n == 5, w_third)
+        when(n == NB - 2, edges2)
         row = back_block(n) * R
         conv = None
-        for j in range(4):
+        for j in range(3):
             part = conv_part(ext2, row, wmat, True, 7 * j, 7 * j + 7)
             conv = part if conv is None else conv + part
-            if j == 3:
-                nat = dot(perm[...], conv.astype(bf16))
-            for t in range((7 * j + 1) // 2, (7 * j + 8) // 2):
+            for t in range(28 * j // 3, 28 * (j + 1) // 3):
                 tap_sums(ext2, row + t // 7 + t % 7, row + t // 7, t % 7, True)
-        for r in range(R):
-            out[row + r] = (cot[row + r].astype(f32) + nat[:, (1 - r) * C:(2 - r) * C]).astype(bf16)
+        for p in range(2):
+            rest = jnp.concatenate([conv_first(ext2, taps, row + 2 * p, o) for o in (1, 0)], axis=-1)
+            last_s[back_block(n) * 2 + p] = (conv[p * COLS:(p + 1) * COLS] + rest).astype(bf16)
         return 0
 
     lax.fori_loop(0, NB, back_step, 0)
-
     @pl.when(lk.top)
     def _():
         for t in range(3):
-            row = ROWS - 3 + t
+            for m in range(t + 1):
+                tap_sums(fold, m, ROWS - 3 + t, 6 - t + m, False)
+
+    rest = [jnp.sum(gks[t], axis=0, keepdims=True) for t in range(49)]
+    rest += [jnp.sum(small[:8], axis=0, keepdims=True), jnp.sum(small[8:], axis=0, keepdims=True), jnp.zeros((13, C), f32)]
+    c3[...] = jnp.concatenate(rest, axis=0).astype(bf16)
+    fan(hop4, N_LON, False)
+    q1[lon] = c3[...]
+
+    def fold_conv():
+        for t in range(3):
             acc = [None] * 16
             for m in range(t + 1):
                 a = 6 - t + m
@@ -568,19 +618,14 @@
                         p = p + fold[m, k + b] * taps[a * 7 + b]
                     p = p.astype(f32)
                     acc[k] = p if acc[k] is None else acc[k] + p
-                tap_sums(fold, m, row, a, False)
-            more = dot(perm[...], jnp.concatenate(acc, axis=0).astype(bf16))
-            out[row] = (out[row].astype(f32) + more).astype(bf16)
-
+            row = ROWS - 3 + t
+            side = slice((1 - row % 2) * C, (2 - row % 2) * C)
+            last_s[row // 2, :, side] = (last_s[row // 2, :, side].astype(f32) + jnp.concatenate(acc, axis=0)).astype(bf16)
+
+    when(lk.top, fold_conv)
+    lax.fori_loop(0, ROWS // 2, finish, 0)
     out_out = pltpu.make_async_copy(out, out_hbm, io.at[0])
     out_out.start()
-
-    c3[...] = jnp.zeros_like(c3)
-    rest = [jnp.sum(gks[t], axis=0, keepdims=True) for t in range(49)]
-    rest += [jnp.sum(small[:8], axis=0, keepdims=True), jnp.sum(small[8:], axis=0, keepdims=True), jnp.zeros((13, C), f32)]
-    c3[...] = jnp.concatenate(rest, axis=0).astype(bf16)
-    fan(hop4, N_LON, False)
-    q1[lon] = c3[...]
     fan(hop3, N_LON, True)
     for j in range(4):
         for k in range(4):
@@ -607,6 +652,11 @@
     out_out.wait()
 
 
+def hand_over(*refs):
+    for a, b in zip(refs[:5], refs[5:]):
+        b[...] = a[...]
+
+
 def body(ocean_state, sea_mask, depth_kernel, conv_bias, norm_gain, w_in, w_out, cotangent):
     cells = COLS * ROWS * lax.axis_size("lat") * lax.axis_size("lon")
     scale = 1.0 / jnp.sqrt(jnp.full((1,), cells, f32))
@@ -625,7 +675,7 @@
             V((ROWS, COLS, C), bf16), V((ROWS, COLS, C), bf16), V((ROWS, COLS, C), bf16),
             V((38, 22, 16, C), bf16), V((38, 22, 16, C), bf16), V((28 * 256, 256), bf16), V((49, 16, C), bf16),
             V((COLS, COLS), bf16), V((96, COLS), bf16), V((96, 32), bf16), V((HID, C), bf16), V((C, HID), bf16),
-            V((2, COLS, R * C), f32),
+            V((2 * COLS, 2 * C), f32), V((R, COLS, C), f32), V((ROWS, COLS, C), bf16), V((ROWS, COLS, C), bf16), V((ROWS // 2, COLS, 2 * C), bf16),
             V((ROWS, 32, C), bf16), V((6, COLS, C), bf16), V((ROWS + 6, 32, C), bf16),
             V((3, 16, 16, C), bf16), V((ROWS + 6, 32, C), bf16), V((3, 22, 16, C), bf16),
             V((C, HID), f32), V((C, HID), f32), V((49, 8, C), f32), V((16, C), f32),
@@ -638,6 +688,14 @@
         compiler_params=pltpu.CompilerParams(collective_id=0, has_side_effects=True, vmem_limit_bytes=VLIM),
         name="block_step",
     )(ocean_state, sea_mask, cotangent, depth_kernel, conv_bias.reshape(1, C), norm_gain.reshape(1, C), w_in, w_out, scale)
+    smalls = (o_k, o_bias, o_gain, o_in, o_out)
+    o_k, o_bias, o_gain, o_in, o_out = pl.pallas_call(
+        hand_over,
+        in_specs=[vm] * 5,
+        out_specs=[vm] * 5,
+        out_shape=[jax.ShapeDtypeStruct(a.shape, a.dtype) for a in smalls],
+        name="hand_over",
+    )(*smalls)
     return upd, grad_state, o_k, o_bias.reshape(C), o_gain.reshape(C), o_in, o_out
 
 

time: 122 us -> 95 us (0.78)
  Pallas kernels: 113 us -> 89.6 us
  local copies, waits for them, and re-layouts: 7.67 us -> 4.61 us
    pallas_call x1, Pallas kernels: 113 us -> 87.7 us  [body(): pl.pallas_call(kernel, in_specs=[vm, vm, hbm, vm, vm, vm, vm, vm, pl.Bloc...]
    unnamed x19 -> x4, local copies, waits for them, and re-layouts: 7.67 us -> 4.61 us
    pallas_call x0 -> x1, Pallas kernels: none -> 1.88 us  [body(): pl.pallas_call(hand_over, in_specs=[vm] * 5, out_specs=[vm] * 5, out_shap...]
where the time goes in v4:
time: 95 us; the launch traced here: 94.9 us
  Pallas kernels  89.6 us (94%)
  local copies, waits for them, and re-layouts  4.61 us (5%)
    pallas_call x1, Pallas kernels, body(): pl.pallas_call(kernel, in_specs=[vm, vm, hbm, vm, vm, vm, vm, vm, pl.Bloc...  87.7 us
    unnamed x4, local copies, waits for them, and re-layouts  4.61 us

profile of v4, /device:TPU:1, one launch (start us, length us, event | category | flops | bytes accessed | tf_op | source)
XLA Modules:
  0.0 94.9 jit_solution(1762859797604856408)
XLA Ops:
  0.6 87.7 %block_step.1 = (bf16[32,256,128]{2,1,0:T(8,128)(2,1)}, bf16[32,256,128]{2,1,0:T(8,128)(2,1)}, f32[128,512]{1,0:T(8,128)}, f32[512,128]{1,0:T(8,128)}, f32[7,7,1...) custom-call(bf16[32,256,128]{2,1,0:T(8,128)(2,1)} %x.1, s32[32,256]{1,0:T(8,128)} %mask.1, ...), custom_call_target="tpu_custom_call" | custom-call | tf_op jit(solution)/shard_map/block_step/pallas_call | solution.py:668
  88.4 1.9 %hand_over.1 = (f32[7,7,128]{2,1,0:T(8,128)}, f32[1,128]{1,0:T(1,128)}, f32[1,128]{1,0:T(1,128)}, f32[128,512]{1,0:T(8,128)}, f32[512,128]{1,0:T(8,128)}) custom-call(f32[7,7,128]{2,1,0:T(8,128)} %get-tuple-element.21.refs_0_, f32[1,128]{1,0:T(1,128)} %get-tuple-element.22.refs_1_, f32[1,128]{1,0:T(1,128)} %get-tuple-element.23.refs_2_, ...), custom_call_target="tpu_custom_call" | custom-call | tf_op jit(solution)/shard_map/hand_over/pallas_call | solution.py:692
  90.3 0.0 copy-start
  90.3 3.3 %copy.17 = bf16[32,256,128]{2,1,0:T(8,128)(2,1)} copy(bf16[32,256,128]{2,1,0:T(8,128)(2,1)} %get-tuple-element.38) | data formatting | bytes 4194304
  93.5 0.0 copy-done
  93.5 1.3 %copy.18 = bf16[32,256,128]{2,1,0:T(8,128)(2,1)} copy(bf16[32,256,128]{2,1,0:T(8,128)(2,1)S(1)} %copy-done) | data formatting | bytes 4194304
Async XLA Ops:
  90.3 3.3 %copy-start = (bf16[32,256,128]{2,1,0:T(8,128)(2,1)S(1)}, bf16[32,256,128]{2,1,0:T(8,128)(2,1)}, u32[]{:S(2)}) copy-start(bf16[32,256,128]{2,1,0:T(8,128)(2,1)} %get-tuple-element.39) | copy-start | bytes 6291460

commit v5 on v4

--- a/solution.py
+++ b/solution.py
@@ -572,7 +572,8 @@
             gks[(48 - t) if flip else t] += q[:8] + q[8:]
 
     def finish(t, _):
-        nat = dot(perm[...], last_s[t])
+        rest = jnp.concatenate([conv_first(ext2, taps, 2 * t, o) for o in (1, 0)], axis=-1)
+        nat = dot(perm[...], (last_s[t].astype(f32) + rest).astype(bf16))
         for o in range(2):
             out[2 * t + o] = (cot[2 * t + o].astype(f32) + nat[:, (1 - o) * C:(2 - o) * C]).astype(bf16)
         return 0
@@ -589,9 +590,9 @@
             conv = part if conv is None else conv + part
             for t in range(28 * j // 3, 28 * (j + 1) // 3):
                 tap_sums(ext2, row + t // 7 + t % 7, row + t // 7, t % 7, True)
+        conv = conv.astype(bf16)
         for p in range(2):
-            rest = jnp.concatenate([conv_first(ext2, taps, row + 2 * p, o) for o in (1, 0)], axis=-1)
-            last_s[back_block(n) * 2 + p] = (conv[p * COLS:(p + 1) * COLS] + rest).astype(bf16)
+            last_s[back_block(n) * 2 + p] = conv[p * COLS:(p + 1) * COLS]
         return 0
 
     lax.fori_loop(0, NB, back_step, 0)
@@ -623,7 +624,15 @@
             last_s[row // 2, :, side] = (last_s[row // 2, :, side].astype(f32) + jnp.concatenate(acc, axis=0)).astype(bf16)
 
     when(lk.top, fold_conv)
-    lax.fori_loop(0, ROWS // 2, finish, 0)
+    lax.fori_loop(0, ROWS // 4, finish, 0)
+    fan(hop4, N_LON, True)
+    total = q1[0].astype(f32)
+    for d in range(1, N_LON):
+        total = total + q1[d].astype(f32)
+    c3[...] = total.astype(bf16)
+    fan(hop5, N_LAT, False)
+    q2[lat] = c3[...]
+    lax.fori_loop(ROWS // 4, ROWS // 2, finish, 0)
     out_out = pltpu.make_async_copy(out, out_hbm, io.at[0])
     out_out.start()
     fan(hop3, N_LON, True)
@@ -632,13 +641,6 @@
             o_in[32 * k:32 * k + 32, j * C:(j + 1) * C] = r3[4 * k + j, 0:32].astype(f32)
         whole = jnp.concatenate([r3[4 * k + j, 32:SEG] for k in range(4)], axis=0).astype(f32)
         o_out[j * C:(j + 1) * C] = whole.T
-    fan(hop4, N_LON, True)
-    total = q1[0].astype(f32)
-    for d in range(1, N_LON):
-        total = total + q1[d].astype(f32)
-    c3[...] = total.astype(bf16)
-    fan(hop5, N_LAT, False)
-    q2[lat] = c3[...]
     fan(hop5, N_LAT, True)
     total = q2[0].astype(f32)
     for d in range(1, N_LAT):
@@ -652,9 +654,26 @@
     out_out.wait()
 
 
-def hand_over(*refs):
-    for a, b in zip(refs[:5], refs[5:]):
+def hand_over(upd, grad, *refs):
+    small, outs = refs[:5], refs[5:12]
+    hold, sin, sout = refs[12:]
+    chunks = [(k, i) for i in range(8) for k in range(2)]
+
+    def move(k, i, inwards):
+        rows = pl.ds(4 * i, 4)
+        if inwards:
+            return pltpu.make_async_copy((upd, grad)[k].at[rows], hold.at[k, rows], sin.at[k, i])
+        return pltpu.make_async_copy(hold.at[k, rows], outs[k].at[rows], sout.at[k, i])
+
+    for k, i in chunks:
+        move(k, i, True).start()
+    for a, b in zip(small, outs[2:]):
         b[...] = a[...]
+    for k, i in chunks:
+        move(k, i, True).wait()
+        move(k, i, False).start()
+    for k, i in chunks:
+        move(k, i, False).wait()
 
 
 def body(ocean_state, sea_mask, depth_kernel, conv_bias, norm_gain, w_in, w_out, cotangent):
@@ -689,13 +708,15 @@
         name="block_step",
     )(ocean_state, sea_mask, cotangent, depth_kernel, conv_bias.reshape(1, C), norm_gain.reshape(1, C), w_in, w_out, scale)
     smalls = (o_k, o_bias, o_gain, o_in, o_out)
-    o_k, o_bias, o_gain, o_in, o_out = pl.pallas_call(
+    upd, grad_state, o_k, o_bias, o_gain, o_in, o_out = pl.pallas_call(
         hand_over,
-        in_specs=[vm] * 5,
-        out_specs=[vm] * 5,
-        out_shape=[jax.ShapeDtypeStruct(a.shape, a.dtype) for a in smalls],
+        in_specs=[hbm, hbm] + [vm] * 5,
+        out_specs=[hbm, hbm] + [vm] * 5,
+        out_shape=[tile, tile] + [jax.ShapeDtypeStruct(a.shape, a.dtype) for a in smalls],
+        scratch_shapes=[V((2, ROWS, COLS, C), bf16), dma((2, 8)), dma((2, 8))],
+        compiler_params=pltpu.CompilerParams(vmem_limit_bytes=VLIM),
         name="hand_over",
-    )(*smalls)
+    )(upd, grad_state, *smalls)
     return upd, grad_state, o_k, o_bias.reshape(C), o_gain.reshape(C), o_in, o_out
 
 

time: 95 us -> 91.7 us (0.965)
  local copies, waits for them, and re-layouts: 4.61 us -> 0 us
  Pallas kernels: 89.6 us -> 90.9 us
    unnamed x4 -> x0, local copies, waits for them, and re-layouts: 4.61 us -> none
    pallas_call x1, Pallas kernels: 1.88 us -> 5.72 us  [body(): pl.pallas_call(hand_over, in_specs=[hbm, hbm] + [vm] * 5, out_specs=[hbm,...]
    pallas_call x1, Pallas kernels: 87.7 us -> 85.2 us  [body(): pl.pallas_call(kernel, in_specs=[vm, vm, hbm, vm, vm, vm, vm, vm, pl.Bloc...]
where the time goes in v5:
time: 91.7 us; the launch traced here: 91.6 us
  Pallas kernels  90.9 us (99%)
    pallas_call x1, Pallas kernels, body(): pl.pallas_call(kernel, in_specs=[vm, vm, hbm, vm, vm, vm, vm, vm, pl.Bloc...  85.2 us
    pallas_call x1, Pallas kernels, body(): pl.pallas_call(hand_over, in_specs=[hbm, hbm] + [vm] * 5, out_specs=[hbm,...  5.72 us

profile of v5, /device:TPU:1, one launch (start us, length us, event | category | flops | bytes accessed | tf_op | source)
XLA Modules:
  0.0 91.6 jit_solution(16919233887066045120)
XLA Ops:
  0.6 85.2 %block_step.1 = (bf16[32,256,128]{2,1,0:T(8,128)(2,1)}, bf16[32,256,128]{2,1,0:T(8,128)(2,1)}, f32[128,512]{1,0:T(8,128)}, f32[512,128]{1,0:T(8,128)}, f32[7,7,1...) custom-call(bf16[32,256,128]{2,1,0:T(8,128)(2,1)} %x.1, s32[32,256]{1,0:T(8,128)} %mask.1, ...), custom_call_target="tpu_custom_call" | custom-call | tf_op jit(solution)/shard_map/block_step/pallas_call | solution.py:687
  85.8 5.7 %hand_over.1 = (bf16[32,256,128]{2,1,0:T(8,128)(2,1)}, bf16[32,256,128]{2,1,0:T(8,128)(2,1)}, f32[7,7,128]{2,1,0:T(8,128)}, f32[1,128]{1,0:T(1,128)}, f32[1,128]...) custom-call(bf16[32,256,128]{2,1,0:T(8,128)(2,1)} %get-tuple-element.21.upd, ...), custom_call_target="tpu_custom_call" | custom-call | tf_op jit(solution)/shard_map/hand_over/pallas_call | solution.py:711
